TPU v7x, 32 devices: a whole 2x2x4 slice. The times are simulated.
32 devices in a mesh: dp: 8 (over z, y), mp: 4 (over x, core).
Axes of the slice: x: 2, y: 2, z: 4, core: 2. Of those that a mesh axis runs over, the one named last changes fastest.
Arguments:
- tokens: bfloat16 [4096, 1024], P('dp'), may hold values from -6 to 6
- cotangent: bfloat16 [4096, 1024], P('dp'), may hold values from -6 to 6
- segment_ids: int32 [4096], P('dp'), may hold values from -1 to 31, as said below
- table_index: int32 [4096], P('dp'), may hold values from 0 to 1043, as said below
- group_count: int32 [8], P('dp'), may hold values from 1 to 4
- owner_list: int32 [192], replicated, may hold values from 0 to 191, each once
- step_count: int32 [1], replicated, may hold values from 2 to 20
- query_weight: bfloat16 [1024, 1024], P(None, 'mp'), may hold values from -0.1875 to 0.1875
- key_weight: bfloat16 [1024, 1024], P(None, 'mp'), may hold values from -0.1875 to 0.1875
- value_weight: bfloat16 [1024, 1024], P(None, 'mp'), may hold values from -0.1875 to 0.1875
- output_weight: bfloat16 [1024, 1024], P('mp'), may hold values from -0.5 to 0.5
- hidden_weight: bfloat16 [1024, 4096], P(None, 'mp'), may hold values from -0.1875 to 0.1875
- return_weight: bfloat16 [4096, 1024], P('mp'), may hold values from -0.09375 to 0.09375
- norm_params: float32 [4, 1024], replicated, may hold values from 0.5 to 1.5
- norm_first: float32 [4, 1024], replicated, may hold values from -0.00390625 to 0.00390625
- norm_second: float32 [4, 1024], replicated, may hold values from 7.9447e-08 to 3.17788e-07
- master_blocks: float32 [192, 4, 128, 128], P('dp', 'mp'), may hold values from -0.1875 to 0.1875
- first_moment: float32 [192, 4, 128, 128], P('dp', 'mp'), may hold values from -0.00390625 to 0.00390625
- second_moment: float32 [192, 4, 128, 128], P('dp', 'mp'), may hold values from 7.9447e-08 to 3.17788e-07
- left_vector: float32 [192, 4, 128], P('dp', 'mp'), may hold values from -6 to 6
- right_vector: float32 [192, 4, 128], P('dp', 'mp'), may hold values from -6 to 6
Outputs:
- layer_output: float32 [4096, 1024], P('dp')
- input_grad: float32 [4096, 1024], P('dp')
- block_grads: float32 [192, 4, 128, 128], P('dp', 'mp')
- block_first: float32 [192, 4, 128, 128], P('dp', 'mp')
- block_second: float32 [192, 4, 128, 128], P('dp', 'mp')
- block_master: float32 [192, 4, 128, 128], P('dp', 'mp')
- block_copy: bfloat16 [192, 4, 128, 128], P('dp', 'mp')
- norm_grads: float32 [2, 4, 1024], replicated
- norm_square: float32 [4, 1024], replicated
- norm_value: float32 [4, 1024], replicated
- clip_norm: float32 [], replicated
Inputs may be any that keep to these rules, and one draw needn't show every extreme that they name: `segment_ids`: on each dp index the items all have one length, 16, 49 or 196 patches, and lie one after another from the first slot, numbered from 0; the slots after them hold -1. Every device holds at least one item. `table_index`: rows 0 to 63 belong to images of 64 patches, 64 to 259 to images of 196, 260 to 1043 to images of 784; all slots of a dp index use the range whose image size matches its item length (64, 196, 784 patches for items of 16, 49, 196). `owner_list`: every block number appears once; slot s lies on dp index s // 24.
All inputs are finite; a program needn't handle non-finite values.
Results may differ from a plain program's by a relative error of at most 0.014.
Values may be sent and summed in bfloat16 or wider, within the bound.
No kernel may reach another device: no remote copies, remote signals or barrier semaphores. Data moves between devices by JAX's collectives and lax.ppermute only.
A program may use at most 128 MiB of HBM per device.

v0:
```python
import functools
import math

import jax
import jax.numpy as jnp
import numpy as np
from jax import lax
from jax.experimental import pallas as pl
from jax.experimental.pallas import tpu as pltpu
from jax.sharding import PartitionSpec as P

D = 1024
HEAD = 64
BLK = 128
LANES = 128
POS_ROWS = 64
SEG_ROWS = 32

clip_max = 1.0
beta_one = 0.5
beta_two = 0.5
adam_eps = 1e-08
step_rate = 0.25
norm_eps = 1e-06
trust_eps = 1e-06

F32 = jnp.float32
BF16 = jnp.bfloat16
MIB = 1024 * 1024
VMEM_LIMIT = 60 * MIB

ERF_P = 0.425
ERF_COEF = (
    0.11983931305209315,
    0.12092032287702306,
    0.10035292560006456,
    0.12754356284084392,
    -0.051626023300101125,
    0.20380940869554587,
    -0.1565787944569494,
    0.035739213095996265,
)


def position_rows():
    coords = np.concatenate(
        [1.75 * np.arange(8), 1.0 * np.arange(14), 0.5 * np.arange(28), np.zeros(POS_ROWS - 50)]
    )
    quarter = D // 4
    freqs = np.power(np.float32(10000.0), -np.arange(quarter, dtype=np.float32) / np.float32(quarter))
    args = (coords.astype(np.float32)[:, None] * freqs.astype(np.float32)[None, :]).astype(np.float64)
    table = np.concatenate([np.sin(args), np.cos(args)], axis=1).astype(np.float32)
    parts = []
    rest = table
    for _ in range(3):
        part = rest.astype(jnp.bfloat16)
        parts.append(part)
        rest = rest - part.astype(np.float32)
    return np.concatenate(parts, axis=0)


def dot_nn(left, right):
    return lax.dot_general(left, right, (((1,), (0,)), ((), ())), preferred_element_type=F32)


def dot_nt(left, right):
    return lax.dot_general(left, right, (((1,), (1,)), ((), ())), preferred_element_type=F32)


def dot_tn(left, right):
    return lax.dot_general(left, right, (((0,), (0,)), ((), ())), preferred_element_type=F32)


def norm_hat(values):
    center = values - jnp.mean(values, axis=-1, keepdims=True)
    inv_std = lax.rsqrt(jnp.mean(center * center, axis=-1, keepdims=True) + norm_eps)
    return (center * inv_std, inv_std)


def norm_back(grad_out, normal, inv_std, gain):
    scaled = grad_out * gain
    return inv_std * (
        scaled
        - jnp.mean(scaled, axis=-1, keepdims=True)
        - normal * jnp.mean(scaled * normal, axis=-1, keepdims=True)
    )


def gelu_parts(values):
    bell = jnp.exp(-0.5 * values * values)
    t = 1.0 / (1.0 + (ERF_P / math.sqrt(2.0)) * jnp.abs(values))
    poly = ERF_COEF[-1]
    for coef in ERF_COEF[-2::-1]:
        poly = poly * t + coef
    tail = poly * t * bell
    dist = jnp.where(values >= 0.0, 1.0 - tail, tail)
    return (values * dist, dist + values * ((1.0 / math.sqrt(2.0 * math.pi)) * bell))


def item_rows(seg_row):
    rows = lax.broadcasted_iota(jnp.int32, (SEG_ROWS, seg_row.shape[1]), 0)
    return jnp.where(rows == seg_row, 1.0, 0.0).astype(BF16)


def head_lanes(rows, head):
    lanes = lax.broadcasted_iota(jnp.int32, (rows, LANES), 1)
    return (lanes // HEAD) == head


def position_hots(index):
    length = index.shape[1]
    big = index >= 260
    mid = index >= 64
    offset = jnp.where(big, 260, jnp.where(mid, 64, 0))
    base = jnp.where(big, 22, jnp.where(mid, 8, 0))
    side = jnp.where(big, 28, jnp.where(mid, 14, 8))
    inv_side = jnp.where(big, 1.0 / 28.0, jnp.where(mid, 1.0 / 14.0, 1.0 / 8.0)).astype(F32)
    local = index - offset
    row = jnp.floor((local.astype(F32) + 0.5) * inv_side).astype(jnp.int32)
    col = local - row * side
    rows = lax.broadcasted_iota(jnp.int32, (3 * POS_ROWS, length), 0) & (POS_ROWS - 1)
    row_hot = jnp.where(rows == base + row, 1.0, 0.0).astype(BF16)
    col_hot = jnp.where(rows == base + col, 1.0, 0.0).astype(BF16)
    return (row_hot, col_hot)


def fill_layer(out_ref, index_row, table, tok_ref, sum_ref=None):
    half = D // 2
    for hot, cols in zip(position_hots(index_row), (slice(0, half), slice(half, D))):
        value = dot_tn(hot, table) + tok_ref[:, cols].astype(F32)
        if sum_ref is not None:
            value = value + sum_ref[:, cols].astype(F32)
        out_ref[:, cols] = value


def fill_bias(bias_ref, seg_row):
    length = seg_row.shape[1]
    items = item_rows(seg_row)
    same = dot_tn(items, items)
    diag = lax.broadcasted_iota(jnp.int32, (length, length), 0) == lax.broadcasted_iota(
        jnp.int32, (length, length), 1
    )
    bias_ref[...] = jnp.where((same > 0.5) | diag, 0.0, -1e30)


def lane_of(values, number):
    lanes = lax.broadcasted_iota(jnp.int32, values.shape, 1)
    return jnp.sum(jnp.where(lanes == number, values, 0.0), axis=1, keepdims=True)


def head_columns(number):
    return pl.ds(pl.multiple_of((number // 2) * LANES, LANES), LANES)


def attend(q_ref, k_ref, v_ref, bias_ref, mixed_ref, lse_ref):
    count = q_ref.shape[0]
    scale = 1.0 / math.sqrt(HEAD)
    step = 512
    for pair in range(q_ref.shape[1] // LANES):
        cols = slice(pair * LANES, (pair + 1) * LANES)
        keys = k_ref[:, cols]
        vals = v_ref[:, cols]
        for at in range(0, count, step):
            rows = slice(at, at + step)
            query = q_ref[rows, cols] * scale
            outs = []
            for head in range(2):
                here = head_lanes(step, head)
                scores = dot_nt(jnp.where(here, query, 0.0).astype(BF16), keys) + bias_ref[rows, :]
                peak = jnp.max(scores, axis=-1, keepdims=True)
                expon = jnp.exp(scores - peak)
                total = jnp.sum(expon, axis=-1, keepdims=True)
                outs.append(dot_nn(expon.astype(BF16), vals) * (1.0 / total))
                number = pair * 2 + head
                lse_ref[rows, number : number + 1] = peak + jnp.log(total)
            mixed_ref[rows, cols] = jnp.where(
                head_lanes(step, 0), outs[0], outs[1]
            ).astype(BF16)


class Load:
    def __init__(self, ref):
        self.ref = ref
        self.copies = []

    def __call__(self):
        for copy in self.copies:
            copy.wait()
        self.copies = []
        return self.ref


class Store:
    def __init__(self, ref, target, sem, running):
        self.ref = ref
        self.target = target
        self.sem = sem
        self.running = running
        self.sent = 0

    def send(self, rows=None):
        source = self.ref if rows is None else self.ref.at[rows]
        target = self.target if rows is None else self.target.at[rows]
        copy = pltpu.make_async_copy(source, target, self.sem.at[self.sent])
        copy.start()
        self.sent += 1
        self.running.append(copy)


    def send_if(self, flag, source):
        @pl.when(flag)
        def _():
            copy = pltpu.make_async_copy(source, self.target, self.sem.at[0])
            copy.start()
            copy.wait()


class Split:
    def __init__(self, ref, keep, send, sem, running, bit):
        self.ref = ref
        self.targets = ((send, 1 - bit), (keep, bit))
        self.sem = sem
        self.running = running

    def send(self):
        half = self.ref.shape[0] // 2
        for i, (target, which) in enumerate(self.targets):
            rows = pl.ds(pl.multiple_of(which * half, half), half)
            copy = pltpu.make_async_copy(self.ref.at[rows], target, self.sem.at[i])
            copy.start()
            self.running.append(copy)


class Rows:
    def __init__(self, array, first, count):
        self.array = array
        self.first = first
        self.count = count


class Into:
    def __init__(self, array, first):
        self.array = array
        self.first = first


class Pair:
    def __init__(self, own, other, first=0, count=None):
        self.own = own
        self.other = other
        self.first = first
        self.count = own.shape[0] if count is None else count


class Stack:
    def __init__(self, *parts):
        self.parts = parts


SEMS = 24


def row_moves(entry, sources, ref, first, bit):
    if isinstance(entry, Stack):
        moves = []
        for part in entry.parts:
            more, first = row_moves(part, sources, ref, first, bit)
            moves += more
        return (moves, first)
    if isinstance(entry, Pair):
        moves = []
        for which in (bit, 1 - bit):
            rows = pl.ds(pl.multiple_of(first + which * entry.count, entry.count), entry.count)
            part = sources.pop(0).at[entry.first : entry.first + entry.count]
            moves.append((part, ref.at[rows]))
        return (moves, first + 2 * entry.count)
    count = entry.count if isinstance(entry, Rows) else entry.shape[0]
    source = sources.pop(0)
    if isinstance(entry, Rows):
        source = source.at[entry.first : entry.first + count]
    whole = count == ref.shape[0]
    return ([(source, ref if whole else ref.at[first : first + count])], first + count)


def flat(entry):
    if isinstance(entry, Stack):
        parts = [flat(part) for part in entry.parts]
        return (sum((p[0] for p in parts), []), sum(p[1] for p in parts), parts[0][2])
    if isinstance(entry, Pair):
        return ([entry.own, entry.other], 2 * entry.count, entry.own)
    if isinstance(entry, Rows):
        return ([entry.array], entry.count, entry.array)
    if isinstance(entry, Into):
        return ([entry.array], entry.first + entry.array.shape[0], entry.array)
    return ([entry], entry.shape[0], entry)


def call(kernel, name, scalars, ins, outs, scratch=(), flops=0, after=None):
    operands = []
    shapes = []
    for entry in ins:
        arrays, rows, like = flat(entry)
        operands += arrays
        shapes.append(((rows,) + like.shape[1:], like.dtype))
    if after is not None:
        operands.append(after)
    results = []
    for shape, kind, *split in outs:
        if split:
            results += [jax.ShapeDtypeStruct((shape[0] // 2,) + shape[1:], kind)] * 2
        else:
            results.append(jax.ShapeDtypeStruct(shape, kind))
    n_scalar, n_in, n_out = len(scalars), len(operands), len(results)

    def body(*refs):
        smem_refs = refs[:n_scalar]
        sources = list(refs[n_scalar : n_scalar + n_in])
        targets = list(refs[n_scalar + n_in : n_scalar + n_in + n_out])
        rest = list(refs[n_scalar + n_in + n_out :])
        in_refs, rest = rest[: len(ins)], rest[len(ins) :]
        out_refs, rest = rest[: len(outs)], rest[len(outs) :]
        in_sem, out_sem = rest[:2]
        bit = smem_refs[0][1] & 1
        loads = []
        number = 0
        for entry, ref in zip(ins, in_refs):
            load = Load(ref)
            if isinstance(entry, Into):
                moves = [(sources.pop(0), ref.at[entry.first : ref.shape[0]])]
            else:
                moves, _ = row_moves(entry, sources, ref, 0, bit)
            for source, target in moves:
                copy = pltpu.make_async_copy(source, target, in_sem.at[number])
                copy.start()
                load.copies.append(copy)
                number += 1
            loads.append(load)
        running = []
        stores = []
        for i, (entry, ref) in enumerate(zip(outs, out_refs)):
            if len(entry) > 2:
                keep, send = targets.pop(0), targets.pop(0)
                stores.append(Split(ref, keep, send, out_sem.at[i], running, bit))
            else:
                stores.append(Store(ref, targets.pop(0), out_sem.at[i], running))
        kernel(*smem_refs, loads, stores, *rest[2:])
        for load in loads:
            load()
        for copy in running:
            copy.wait()

    hbm = pl.BlockSpec(memory_space=pltpu.HBM)
    return pl.pallas_call(
        body,
        name=name,
        out_shape=results,
        in_specs=[pl.BlockSpec(memory_space=pltpu.SMEM)] * n_scalar + [hbm] * n_in,
        out_specs=[hbm] * n_out,
        scratch_shapes=[pltpu.VMEM(shape, kind) for shape, kind in shapes]
        + [pltpu.VMEM(shape, kind) for shape, kind, *_ in outs]
        + [pltpu.SemaphoreType.DMA((max(n_in, 1),)), pltpu.SemaphoreType.DMA((len(outs), SEMS))]
        + [pltpu.VMEM(shape, kind) for shape, kind in scratch],
        compiler_params=pltpu.CompilerParams(vmem_limit_bytes=VMEM_LIMIT),
        cost_estimate=pl.CostEstimate(flops=int(flops), bytes_accessed=0, transcendentals=0),
    )(*scalars, *operands)


def forward_kernel(me_ref, loads, stores, layer_ref, bias_ref):
    index, table, tokens, seg, norm, wq, wk, wv, wo = loads
    normed, q, k, v, mixed, lse, first, last = stores
    length = tokens.ref.shape[0]
    half = length // 2
    index_row = index()[...]
    rows_of = table()[...]
    tok_ref = tokens()
    fill_layer(layer_ref, index_row, rows_of, tok_ref)
    fill_bias(bias_ref, seg()[...])
    norm_ref = norm()
    step = 128
    for at in range(0, length, step):
        rows = slice(at, at + step)
        hat, _ = norm_hat(layer_ref[rows, :])
        normed.ref[rows, :] = (hat * norm_ref[0:1, :] + norm_ref[1:2, :]).astype(BF16)
    normed.send()
    left = normed.ref[...]
    for weight, out in ((wq, q), (wk, k), (wv, v)):
        out.ref[...] = dot_nn(left, weight()[...]).astype(BF16)
        out.send()
    attend(q.ref, k.ref, v.ref, bias_ref, mixed.ref, lse.ref)
    mixed.send()
    lse.send()
    wo_ref = wo()
    for at, out in ((0, first), (half, last)):
        out.ref[...] = dot_nn(mixed.ref[at : at + half, :], wo_ref[...]).astype(BF16)
        out.send()


def grad_out_kernel(me_ref, loads, stores):
    seg, cotangent, return_weight = loads
    gout, gact = stores
    items = item_rows(seg()[...])
    valid = dot_tn(items, jnp.ones((SEG_ROWS, LANES), BF16))
    cot_ref = cotangent()
    for at in range(0, D, LANES):
        cols = slice(at, at + LANES)
        gout.ref[:, cols] = (cot_ref[:, cols].astype(F32) * valid).astype(BF16)
    gout.send()
    weight = return_weight()[...]
    half = gact.ref.shape[0] // 2
    for at in (0, half):
        rows = slice(at, at + half)
        gact.ref[rows, :] = dot_nt(gout.ref[rows, :], weight)
        gact.send(rows)


def feed_kernel(row0, me_ref, loads, stores, pre_ref):
    index, table, tokens, sums, norm, hidden_weight, gact = loads
    second, act, gpre, part = stores
    length = tokens.ref.shape[0]
    index_row = index()[:, row0 : row0 + length]
    rows_of = table()[...]
    tok_ref = tokens()
    fill_layer(pre_ref, index_row, rows_of, tok_ref, sums())
    norm_ref = norm()
    step = 64
    for at in range(0, length, step):
        rows = slice(at, at + step)
        hat, _ = norm_hat(pre_ref[rows, :])
        second.ref[rows, :] = (hat * norm_ref[2:3, :] + norm_ref[3:4, :]).astype(BF16)
    second.send()
    weight_ref = hidden_weight()
    pre_ref[...] = dot_nn(second.ref[...], weight_ref[...])
    gact_ref = gact()
    step = 32

    @pl.loop(0, length // step)
    def _(i):
        rows = pl.ds(pl.multiple_of(i * step, step), step)
        value, slope = gelu_parts(pre_ref[rows, :])
        act.ref[rows, :] = value.astype(BF16)
        gpre.ref[rows, :] = (gact_ref[rows, :] * slope).astype(BF16)

    act.send()
    gpre.send()
    part.ref[...] = dot_nt(gpre.ref[...], weight_ref[...]).astype(BF16)
    part.send()


def store_blocks(nat_ref, base, left, right_ref, weight):
    width = right_ref.shape[1]
    across = width // BLK
    wide = 256

    @pl.loop(0, width // wide)
    def _(step):
        cols = pl.ds(pl.multiple_of(step * wide, wide), wide)
        grad = (dot_tn(left, right_ref[:, cols]) * weight).astype(BF16)
        for i in range(grad.shape[0] // BLK):
            for j in range(wide // BLK):
                nat_ref[base + i * across + step * (wide // BLK) + j] = grad[
                    i * BLK : (i + 1) * BLK, j * BLK : (j + 1) * BLK
                ]


def relative(order, bits):
    out = 0
    for i, bit in enumerate(bits):
        if (order >> (len(bits) - 1 - i)) & 1:
            out |= bit
    return out


def gather_blocks(me_ref, source_ref, positions, first, count, bits, keep_ref, send_ref, block_at):
    owners = 2 ** len(bits)
    for order in range(owners):
        dest = me_ref[0] ^ relative(order, bits)
        out_ref = keep_ref if order < owners // 2 else send_ref
        at = (order % (owners // 2)) * count

        @pl.loop(0, count)
        def _(j, out_ref=out_ref, at=at, place=dest * positions + first):
            out_ref[at + j] = block_at(source_ref[place + j])


def feed_grad_kernel(
    bits, early_slots, positions, late_count, me_ref, source_ref, scal_ref, loads, stores, nat_ref
):
    second, gpre, act, gout = loads
    rest = stores[0]
    weight = scal_ref[0]
    store_blocks(nat_ref, 0, second()[...], gpre(), weight)
    store_blocks(nat_ref, 64, act()[...], gout(), weight)

    def block_at(block):
        return nat_ref[jnp.maximum(block - late_count, 0)]

    if early_slots:
        keep, send = stores[1:]
        gather_blocks(
            me_ref, source_ref, positions, 0, early_slots, bits, keep.ref, send.ref, block_at
        )
        send.send()
        keep.send()

    @pl.loop(0, rest.ref.shape[0])
    def _(i):
        rest.ref[i] = block_at(source_ref[2 ** len(bits) * positions + i])

    rest.send()


def backward_kernel(
    chunks,
    first,
    positions,
    late_count,
    me_ref,
    source_ref,
    scal_ref,
    loads,
    stores,
    gattn_ref,
    gmix_ref,
    grads_ref,
    hid_ref,
    bias_ref,
):
    index, table, tokens, attn, norm, sums, gout = loads[:7]
    wo, seg, q, k, v, lse, normed, mixed, rest, qkv_weight, act, return_weight = loads[7:]
    late, parts = stores[:2]
    chunk_stores = stores[2:]
    length = tokens.ref.shape[0]
    half = length // 2
    width = q.ref.shape[1]
    weight = scal_ref[0]
    step = 64
    index_row, rows_of, tok_ref = index()[...], table()[...], tokens()
    fill_layer(hid_ref, index_row, rows_of, tok_ref, attn())
    norm_ref, gout_ref, sum_ref = norm(), gout(), sums()

    @pl.loop(0, length // step, unroll=2)
    def _(i):
        rows = pl.ds(pl.multiple_of(i * step, step), step)
        hat, inv_std = norm_hat(hid_ref[rows, :])
        grad = sum_ref[rows, :].astype(F32)
        value = gout_ref[rows, :].astype(F32) + norm_back(grad, hat, inv_std, norm_ref[2:3, :])
        gattn_ref[rows, :] = value.astype(BF16)

    fill_bias(bias_ref, seg()[...])
    gmix_ref[...] = dot_nt(gattn_ref[...], wo()[...]).astype(BF16)
    scale = 1.0 / math.sqrt(HEAD)
    q_ref, k_ref, v_ref, lse_ref = q(), k(), v(), lse()

    @pl.loop(0, q_ref.shape[1] // HEAD)
    def _(number):
        cols = head_columns(number)
        here = head_lanes(length, number % 2)
        keys, vals = k_ref[:, cols], v_ref[:, cols]
        query = q_ref[:, cols] * scale
        gmix = gmix_ref[:, cols]
        scores = dot_nt(jnp.where(here, query, 0.0).astype(BF16), keys) + bias_ref[...]
        probs = jnp.exp(scores - lane_of(lse_ref[...], number))
        grad_probs = dot_nt(jnp.where(here, gmix, 0.0).astype(BF16), vals)
        grad_scores = (
            probs * (grad_probs - jnp.sum(probs * grad_probs, axis=-1, keepdims=True))
        ).astype(BF16)
        for place, value in (
            (2, dot_tn(probs.astype(BF16), gmix)),
            (1, dot_tn(grad_scores, query)),
            (0, dot_nn(grad_scores, keys) * scale),
        ):
            old = grads_ref[place, :, cols]
            grads_ref[place, :, cols] = jnp.where(here, value.astype(BF16), old)

    weights_ref, act_ref, return_ref = qkv_weight(), act(), return_weight()

    @pl.loop(0, 2)
    def _(i):
        rows = pl.ds(pl.multiple_of(i * half, half), half)
        total = sum(
            dot_nt(grads_ref[place, rows, :], weights_ref[place * D : (place + 1) * D, :])
            for place in range(3)
        )
        parts.ref[pl.ds(pl.multiple_of(2 * i * half, half), half), :] = total.astype(BF16)
        parts.ref[pl.ds(pl.multiple_of((2 * i + 1) * half, half), half), :] = dot_nn(
            act_ref[rows, :], return_ref[...]
        ).astype(BF16)

    parts.send()
    pool_ref = rest.ref
    left = normed()[...]
    share = D // BLK * (width // BLK)

    @pl.loop(0, 3)
    def _(place):
        store_blocks(pool_ref, place * share, left, grads_ref.at[place], weight)

    store_blocks(pool_ref, 3 * share, mixed()[...], gattn_ref, weight)
    rest()
    for number, (count, bits) in enumerate(chunks):
        keep, send = chunk_stores[2 * number : 2 * number + 2]
        gather_blocks(
            me_ref,
            source_ref,
            positions,
            first,
            count,
            bits,
            keep.ref,
            send.ref,
            lambda place: pool_ref[place],
        )
        send.send()
        keep.send()
        first += count
    late.send_if(scal_ref[3] > 0.5, pool_ref.at[0:late_count])


def overflow_kernel(first, count, bits, positions, me_ref, source_ref, loads, stores):
    (late,) = loads
    keep, send = stores
    late_ref = late()
    last = late_ref.shape[0] - 1
    gather_blocks(
        me_ref,
        source_ref,
        positions,
        first,
        count,
        bits,
        keep.ref,
        send.ref,
        lambda place: late_ref[jnp.minimum(place, last)],
    )
    keep.send()
    send.send()


def add_rows(acc_ref, at, values):
    acc_ref[at : at + 8, :] += jnp.sum(values.reshape(values.shape[0] // 8, 8, D), axis=0)


def finish_kernel(me_ref, scal_ref, loads, stores, layer_ref, acc_ref):
    index, table, tokens, attn_a, attn_b, norm, outputs, second_a, second_b, gout = loads
    out, gin, sums = stores
    half = attn_a.ref.shape[0]
    weight = scal_ref[0]
    step = 64
    acc_ref[...] = jnp.zeros_like(acc_ref)
    index_row = index()[...]
    rows_of = table()[...]
    tok_ref = tokens()
    for row0, attn, second in ((0, attn_a, second_a), (half, attn_b, second_b)):
        part = slice(row0, row0 + half)
        fill_layer(layer_ref, index_row[:, part], rows_of, tok_ref.at[part, :])
        attn_ref, norm_ref, second_ref, gout_ref, both_ref = (
            attn(),
            norm(),
            second(),
            gout(),
            outputs(),
        )
        @pl.loop(0, half // step)
        def _(
            i,
            row0=row0,
            attn_ref=attn_ref,
            norm_ref=norm_ref,
            second_ref=second_ref,
            gout_ref=gout_ref,
            both_ref=both_ref,
        ):
            at = pl.multiple_of(i * step, step)
            here = pl.ds(at, step)
            rows = pl.ds(pl.multiple_of(row0 + at, step), step)
            first_at = pl.multiple_of(2 * row0 + at, step)
            layer = layer_ref[here, :]
            hat, inv_std = norm_hat(layer)
            hid = layer + attn_ref[here, :].astype(F32)
            mlp = both_ref[pl.ds(first_at + half, step), :].astype(F32)
            out.ref[rows, :] = hid + mlp
            hat2, inv_std2 = norm_hat(hid)
            grad2 = second_ref[here, :].astype(F32)
            ghid = gout_ref[rows, :].astype(F32) + norm_back(
                grad2, hat2, inv_std2, norm_ref[2:3, :]
            )
            add_rows(acc_ref, 16, grad2 * hat2)
            add_rows(acc_ref, 24, grad2)
            grad = both_ref[pl.ds(first_at, step), :].astype(F32)
            gin.ref[rows, :] = ghid + norm_back(grad, hat, inv_std, norm_ref[0:1, :])
            add_rows(acc_ref, 0, grad * hat)
            add_rows(acc_ref, 8, grad)

        out.send(part)
        gin.send(part)
    for i in range(4):
        sums.ref[i : i + 1, :] = (
            jnp.sum(acc_ref[8 * i : 8 * i + 8, :], axis=0, keepdims=True) * weight
        )
    sums.ref[4:5, :] = jnp.full((1, D), weight, F32)
    sums.ref[5:8, :] = jnp.zeros((3, D), F32)
    sums.send()


def columns(rows):
    count = rows.shape[0]
    if count % 8:
        return jnp.stack(
            [jnp.transpose(jnp.broadcast_to(rows[i : i + 1], (BLK, BLK)))[:, 0:1] for i in range(count)]
        )
    turned = jnp.transpose(rows)
    return jnp.stack([turned[:, i : i + 1] for i in range(count)])


def reflect(blocks, left, right, coef_left, coef_right):
    along = jnp.sum(left * blocks, axis=1, keepdims=True) * coef_left
    blocks = blocks - left * along
    across = jnp.sum(blocks * right, axis=2, keepdims=True) * coef_right
    return blocks - across * right


def reflectors(left_ref, right_ref):
    left, right = left_ref[...], right_ref[...]
    coef_left = (2.0 / jnp.sum(left * left, axis=1, keepdims=True))[:, :, None]
    coef_right = (2.0 / jnp.sum(right * right, axis=1, keepdims=True))[:, :, None]
    return (columns(left), right[:, None, :], coef_left, coef_right)


def rotate_kernel(counts, group, me_ref, place_ref, loads, stores, found_ref):
    left, right = loads[:2]
    grads, turned, total = stores
    parts = reflectors(left(), right())
    at = 0
    for number, count in enumerate(counts):
        keep, got = loads[2 + 2 * number : 4 + 2 * number]
        found_ref[at : at + count] = keep()[...].astype(F32) + got()[...].astype(F32)
        at += count
    slots = grads.ref.shape[0]
    for slot in range(slots):
        grads.ref[slot] = found_ref[place_ref[me_ref[0] * slots + slot]]
    grads.send()
    square = jnp.zeros((8, BLK), F32)
    for at in range(0, slots, group):
        rows = slice(at, at + group)
        grad = grads.ref[rows]
        square = square + jnp.sum((grad * grad).reshape(group * BLK // 8, 8, BLK), axis=0)
        turned.ref[rows] = reflect(grad, *(part[rows] for part in parts))
        turned.send(rows)
    total.ref[...] = jnp.full((8, BLK), jnp.sum(square), F32)
    total.send()


def inverse(value):
    guess = pl.reciprocal(value, approx=True)
    return guess * (2.0 - value * guess)


def update_kernel(group, me_ref, scal_ref, loads, stores):
    sums, norm, norm_first, norm_second, left, right = loads[:6]
    grads, turned_grads, old_first, old_second, old_master = loads[6:]
    out_grad, out_first, out_second, out_master, out_copy = stores[:5]
    norm_pair, norm_square, norm_value, clip_out = stores[5:]
    inv_one = 1.0 / scal_ref[1]
    inv_two = 1.0 / scal_ref[2]
    sums_ref = sums()
    share = 1.0 / sums_ref[4:5, 0:BLK]
    norm_grad = sums_ref[0:4, :] * share[:, 0:1]
    total = sums_ref[5:6, 0:BLK] * (share * share) + jnp.sum(norm_grad * norm_grad)
    clip_norm = jnp.sqrt(total)
    clip = jnp.minimum(1.0, clip_max / clip_norm)
    factor = (share * clip)[:, None, :]
    parts = reflectors(left(), right())
    slots = left.ref.shape[0]
    entries = 1.0 / (BLK * BLK)
    for at in range(0, slots, group):
        rows = slice(at, at + group)
        out_grad.ref[rows] = grads()[rows] * factor
        rotated = turned_grads()[rows] * factor
        first = beta_one * old_first()[rows] + (1.0 - beta_one) * rotated
        second = beta_two * old_second()[rows] + (1.0 - beta_two) * rotated * rotated
        out_first.ref[rows] = first
        out_second.ref[rows] = second
        spread = second * inv_two
        normal = (first * inv_one) * inverse(spread * lax.rsqrt(spread) + adam_eps)
        turned = reflect(normal, *(part[rows] for part in parts))
        master = old_master()[rows]
        size = jnp.sum(jnp.sum(master * master, axis=1, keepdims=True), axis=2, keepdims=True)
        move = jnp.sum(jnp.sum(turned * turned, axis=1, keepdims=True), axis=2, keepdims=True)
        trust = jnp.sqrt(size * entries + trust_eps) / jnp.sqrt(move * entries + trust_eps)
        fresh = master - (step_rate * trust) * turned
        out_master.ref[rows] = fresh
        out_copy.ref[rows] = fresh.astype(BF16)
        for out in (out_grad, out_first, out_second, out_master, out_copy):
            out.send(rows)
    clip_out.ref[...] = jnp.broadcast_to(clip_norm, clip_out.ref.shape)
    clip_out.send()
    clipped = norm_grad * clip[:, 0:1]
    first = beta_one * norm_first()[...] + (1.0 - beta_one) * clipped
    second = beta_two * norm_second()[...] + (1.0 - beta_two) * clipped * clipped
    norm_pair.ref[0] = clipped
    norm_pair.ref[1] = first
    norm_pair.send()
    norm_square.ref[...] = second
    norm_square.send()
    norm_value.ref[...] = norm()[...] - step_rate * (first * inv_one) / (
        jnp.sqrt(second * inv_two) + adam_eps
    )
    norm_value.send()


def swap(value, axis, bit):
    count = lax.axis_size(axis)
    return lax.ppermute(value, axis, [(i, i ^ bit) for i in range(count)])


def plus(left, right):
    return (left.astype(F32) + right.astype(F32)).astype(BF16)


def after(value, *others):
    return lax.optimization_barrier((value, *others))[0]


def mp_far(total, wait=None):
    bit = 2
    while bit < lax.axis_size("mp"):
        got = swap(total, "mp", bit)
        total = plus(total, got if wait is None else after(got, wait))
        bit *= 2
    return total


def mp_sum(keep, send):
    total = mp_far(plus(keep, swap(send, "mp", 1)))
    return (total, swap(total, "mp", 1))


def early_count(slots):
    return slots // 3 if slots >= 24 else 0


def split_counts(slots, bits):
    if slots >= 8:
        last = slots // 4
        head = (slots - last + 2) // 2
        crossed = (bits[1], bits[0]) + bits[2:]
        return ((head, bits), (slots - last - head, bits), (last, crossed))
    return ((1, bits),) * slots if slots <= 3 else ((slots - slots // 2, bits), (slots // 2, bits))


def exclusive_sum(values):
    size = values.shape[-1]
    before = jnp.asarray(np.tril(np.ones((size, size), np.int32), -1))
    return jnp.sum(values[..., None, :] * before, axis=-1)


def rest_count(blocks, late_count, n_dp, slots, early_slots):
    total = blocks - late_count
    full, over = divmod(total, slots)
    return total - full * early_slots - min(over, early_slots)


def slot_tables(owner_list, n_dp, slots, early_slots, late_count):
    blocks = owner_list.shape[0]
    owned = owner_list.reshape(n_dp, slots)
    early = (owned >= late_count).astype(jnp.int32)
    if early_slots:
        goes = early * (exclusive_sum(early) < early_slots).astype(jnp.int32)
        place = jnp.where(goes == 1, exclusive_sum(early), early_slots + exclusive_sum(1 - goes))
        positions = slots + early_slots
        hit = place[:, None, :] == jnp.arange(positions, dtype=jnp.int32)[None, :, None]
        source = jnp.sum(jnp.where(hit, owned[:, None, :], 0), axis=2)
        short = jnp.any(jnp.sum(early, axis=1) < early_slots)
    else:
        place = jnp.broadcast_to(jnp.arange(slots, dtype=jnp.int32), (n_dp, slots))
        source, short = owned, jnp.zeros((), bool)
    later = source[:, early_slots:].reshape(-1)
    is_rest = (later >= late_count).astype(jnp.int32)
    order = exclusive_sum(is_rest)
    count = rest_count(blocks, late_count, n_dp, slots, early_slots)
    hit = (order[None, :] == jnp.arange(count, dtype=jnp.int32)[:, None]) & (is_rest[None, :] == 1)
    rest = jnp.sum(jnp.where(hit, later[None, :], 0), axis=1)
    later = jnp.where(is_rest == 1, late_count + order, later)
    source = jnp.concatenate([source[:, :early_slots], later.reshape(n_dp, -1)], axis=1)
    return (jnp.concatenate([source.reshape(-1), rest]), place.reshape(-1), short)


def shards(
    tokens,
    cotangent,
    segment_ids,
    table_index,
    group_count,
    owner_list,
    step_count,
    query_weight,
    key_weight,
    value_weight,
    output_weight,
    hidden_weight,
    return_weight,
    norm_params,
    norm_first,
    norm_second,
    master_blocks,
    first_moment,
    second_moment,
    left_vector,
    right_vector,
):
    length = tokens.shape[0]
    half = length // 2
    width = query_weight.shape[1]
    heads = width // HEAD
    units = hidden_weight.shape[1]
    slots = master_blocks.shape[0]
    blocks = owner_list.shape[0]
    late_count = blocks // 3
    n_dp = lax.axis_size("dp")
    natural = tuple(1 << i for i in range(n_dp.bit_length() - 1))
    early_slots = early_count(slots)
    positions = slots + early_slots
    me = jnp.stack([lax.axis_index("dp"), lax.axis_index("mp")]).astype(jnp.int32)
    step_value = step_count[0].astype(F32)
    source, place, short = slot_tables(owner_list, n_dp, slots, early_slots, late_count)
    scal = jnp.stack(
        [
            group_count[0].astype(F32),
            1.0 - jnp.power(beta_one, step_value),
            1.0 - jnp.power(beta_two, step_value),
            short.astype(F32),
        ]
    )
    seg_row = segment_ids.reshape(1, length)
    index_row = table_index.reshape(1, length)
    table = jnp.asarray(position_rows())
    rows_d = (length, D)
    half_d = (half, D)
    unit = 2 * length * D * D
    wide = ((length, width), BF16)

    normed, q, k, v, mixed, lse, keep_a, send_a, keep_b, send_b = call(
        forward_kernel,
        "attention_forward",
        (me,),
        (
            index_row,
            table,
            tokens,
            seg_row,
            norm_params,
            query_weight,
            key_weight,
            value_weight,
            output_weight,
        ),
        [
            (rows_d, BF16),
            wide,
            wide,
            wide,
            wide,
            ((length, heads), F32),
            (half_d, BF16, True),
            (half_d, BF16, True),
        ],
        [(rows_d, F32), ((length, length), F32)],
        flops=5 * unit,
    )
    near_a = plus(keep_a, swap(send_a, "mp", 1))
    near_b = plus(keep_b, swap(send_b, "mp", 1))
    token = near_b
    grad_out, grad_act = call(
        grad_out_kernel,
        "grad_of_act",
        (me,),
        (seg_row, cotangent, return_weight),
        [(rows_d, BF16), ((length, units), F32)],
        flops=2 * unit,
        after=token,
    )

    far_a = mp_far(near_a, grad_act)
    attn_a = Pair(far_a, swap(far_a, "mp", 1))
    def feed(row0, name, sums, token):
        return call(
            functools.partial(feed_kernel, row0),
            name,
            (me,),
            (
                index_row,
                table,
                Rows(tokens, row0, half),
                sums,
                norm_params,
                hidden_weight,
                Rows(grad_act, row0, half),
            ),
            [
                (half_d, BF16),
                ((half, units), BF16),
                ((half, units), BF16),
                (half_d, BF16, True),
            ],
            [((half, units), F32)],
            flops=4 * unit,
            after=token,
        )

    second_a, act_a, gpre_a, keep_a, send_a = feed(0, "feed_forward_a", attn_a, None)
    far_b = mp_far(near_b, keep_a)
    attn_b = Pair(far_b, swap(far_b, "mp", 1))
    second_b, act_b, gpre_b, keep_b, send_b = feed(half, "feed_forward_b", attn_b, keep_a)
    near_a = plus(keep_a, swap(send_a, "mp", 1))
    near_b = plus(keep_b, swap(send_b, "mp", 1))
    far_a = mp_far(near_a, near_b)
    chunk_e = [((n_dp // 2 * early_slots, BLK, BLK), BF16)] * 2 if early_slots else []
    count = rest_count(blocks, late_count, n_dp, slots, early_slots)
    rest, *chunk_e = call(
        functools.partial(feed_grad_kernel, natural, early_slots, positions, late_count),
        "feed_weight_grads",
        (me, source, scal),
        (Stack(second_a, second_b), Stack(gpre_a, gpre_b), Stack(act_a, act_b), grad_out),
        [((count, BLK, BLK), BF16)] + chunk_e,
        [((blocks - late_count, BLK, BLK), BF16)],
        flops=4 * unit,
        after=near_b,
    )
    far_b = mp_far(near_b, rest)
    sum_a = Pair(far_a, swap(far_a, "mp", 1))
    sum_b = Pair(far_b, swap(far_b, "mp", 1))
    got_e = swap(chunk_e[1], "dp", 1) if early_slots else None
    chunks = split_counts(slots - early_slots, natural)
    chunk_shapes = []
    for count, _ in chunks:
        chunk_shapes += [((n_dp // 2 * count, BLK, BLK), BF16)] * 2
    outs = call(
        functools.partial(backward_kernel, chunks, early_slots, positions, late_count),
        "attention_backward",
        (me, source, scal),
        (
            index_row,
            table,
            tokens,
            Stack(attn_a, attn_b),
            norm_params,
            Stack(sum_a, sum_b),
            grad_out,
            output_weight,
            seg_row,
            q,
            k,
            v,
            lse,
            normed,
            mixed,
            Into(rest, late_count),
            Stack(query_weight, key_weight, value_weight),
            Stack(act_a, act_b),
            return_weight,
        ),
        [((late_count, BLK, BLK), BF16), ((2 * length, D), BF16, True)] + chunk_shapes,
        [(rows_d, BF16)]
        + [((length, width), BF16), ((3, length, width), BF16)]
        + [(rows_d, F32), ((length, length), F32)],
        flops=10 * unit,
    )
    late, keep, send = outs[:3]
    queue = [(outs[3 + 2 * i], outs[4 + 2 * i]) for i in range(len(chunks))]
    counts = [count for count, _ in chunks]
    orders = [bits for _, bits in chunks]

    stages = len(natural)
    state = [(first, swap(second, "dp", bits[0])) for (first, second), bits in zip(queue, orders)]
    if early_slots:
        state.insert(0, (chunk_e[0], after(got_e, keep)))
        counts.insert(0, early_slots)
        orders.insert(0, natural)
    level = [0] * len(state)
    last = []

    def in_turn(got):
        got = after(got, *last)
        last[:] = [got]
        return got

    def halve(number):
        keep, got = state[number]
        got = in_turn(got)
        if level[number] < stages - 1:
            n = keep.shape[0] // 2
            keep, send = plus(keep[:n], got[:n]), plus(keep[n:], got[n:])
            got = swap(send, "dp", orders[number][level[number] + 1])
            last.append(send)
        level[number] += 1
        state[number] = (keep, got)

    def mp_first(keep, send):
        return plus(keep, in_turn(swap(send, "mp", 1)))

    def mp_rest(near):
        bit = 2
        while bit < lax.axis_size("mp"):
            near = plus(near, in_turn(swap(near, "mp", bit)))
            bit *= 2
        return Pair(near, swap(near, "mp", 1))

    if early_slots:
        halve(0)
    def finish(both):
        outputs = call(
            finish_kernel,
            "layer_outputs",
            (me, scal),
            (
                index_row,
                table,
                tokens,
                attn_a,
                attn_b,
                norm_params,
                both,
                sum_a,
                sum_b,
                grad_out,
            ),
            [(rows_d, F32), (rows_d, F32), ((8, D), F32)],
            [(half_d, F32), ((32, D), F32)],
            flops=2 * unit,
        )
        last.append(outputs[2])
        return outputs

    plan = ["near", "far", "finish"]
    if early_slots and stages == 3:
        plan = ["near",(3,0),(1,0),(0,1),(2,0),(1,1),(3,1),(0,2),(2,1),(1,2),"far","finish"]
    plan += [(i, d - i) for d in range(len(state) + stages) for i in range(len(state))]
    for entry in plan:
        if entry == "near":
            near = plus(keep, in_turn(swap(send, "mp", 1)))
        elif entry == "far":
            bit = 2
            while bit < lax.axis_size("mp"):
                near = plus(near, in_turn(swap(near, "mp", bit)))
                bit *= 2
            both = Pair(near, swap(near, "mp", 1))
        elif entry == "finish":
            out, input_grad, sums = finish(both)
        elif level[entry[0]] == entry[1] < stages:
            halve(entry[0])
    pending = [array for pair in state for array in pair]

    if early_slots:
        shape = (n_dp // 2 * early_slots, BLK, BLK)

        def exchange(late):
            keep, send = call(
                functools.partial(overflow_kernel, slots, early_slots, natural, positions),
                "overflow",
                (me, source),
                (late,),
                [(shape, BF16), (shape, BF16)],
            )
            bit = 1
            while True:
                got = swap(send, "dp", bit)
                bit *= 2
                if bit >= n_dp:
                    return (keep, got)
                n = keep.shape[0] // 2
                keep, send = plus(keep[:n], got[:n]), plus(keep[n:], got[n:])

        def nothing(late):
            zero = jnp.zeros((early_slots, BLK, BLK), BF16)
            return (zero, zero)

        pending += list(lax.cond(short, exchange, nothing, late))
        counts.append(early_slots)

    left = left_vector.reshape(slots, BLK)
    right = right_vector.reshape(slots, BLK)
    block_f32 = ((slots, BLK, BLK), F32)
    group = 4 if slots % 4 == 0 else 1
    grads, rotated, square = call(
        functools.partial(rotate_kernel, counts, group),
        "rotate",
        (me, place),
        (left, right, *pending),
        [block_f32, block_f32, ((8, BLK), F32)],
        [((sum(counts), BLK, BLK), F32)],
        flops=unit,
    )
    bit = 1
    while bit < lax.axis_size("mp"):
        square = square + swap(square, "mp", bit)
        bit *= 2
    sums = sums + jnp.pad(square[0:1], ((5, 2), (0, D - BLK)))
    bit = 1
    while bit < n_dp:
        sums = sums + swap(sums, "dp", bit)
        bit *= 2
    new = call(
        functools.partial(update_kernel, group),
        "update",
        (me, scal),
        (
            sums,
            norm_params,
            norm_first,
            norm_second,
            left,
            right,
            grads,
            rotated,
            first_moment.reshape(slots, BLK, BLK),
            second_moment.reshape(slots, BLK, BLK),
            master_blocks.reshape(slots, BLK, BLK),
        ),
        [block_f32] * 4
        + [
            ((slots, BLK, BLK), BF16),
            ((2, 4, D), F32),
            ((4, D), F32),
            ((4, D), F32),
            ((8, BLK), F32),
        ],
        flops=unit,
    )
    shard_shape = (slots, 1, BLK, BLK)
    return (
        out,
        input_grad,
        new[0].reshape(shard_shape),
        new[1].reshape(shard_shape),
        new[2].reshape(shard_shape),
        new[3].reshape(shard_shape),
        new[4].reshape(shard_shape),
        new[5],
        new[6],
        new[7],
        new[8][0, 0],
    )


def solution(mesh):
    placed = (
        P("dp", None),
        P("dp", None),
        P("dp"),
        P("dp"),
        P("dp"),
        P(),
        P(),
        P(None, "mp"),
        P(None, "mp"),
        P(None, "mp"),
        P("mp", None),
        P(None, "mp"),
        P("mp", None),
        P(),
        P(),
        P(),
        P("dp", "mp", None, None),
        P("dp", "mp", None, None),
        P("dp", "mp", None, None),
        P("dp", "mp", None),
        P("dp", "mp", None),
    )
    return jax.shard_map(
        shards,
        mesh=mesh,
        in_specs=placed,
        out_specs=(
            P("dp", None),
            P("dp", None),
            P("dp", "mp", None, None),
            P("dp", "mp", None, None),
            P("dp", "mp", None, None),
            P("dp", "mp", None, None),
            P("dp", "mp", None, None),
            P(),
            P(),
            P(),
            P(),
        ),
        check_vma=False,
    )
```

profile of v0, /device:TPU:0, one launch (start us, length us, event | category | flops | bytes accessed | tf_op | source)
XLA Modules:
  0.0 198.9 jit_solution(199267780625919702)
XLA Ops:
  0.7 10.2 %attention_forward.1 = (bf16[512,1024]{1,0:T(8,128)(2,1)}, bf16[512,256]{1,0:T(8,128)(2,1)}, bf16[512,256]{1,0:T(8,128)(2,1)}, bf16[512,256]{1,0:T(8,128)(2,1)},...) custom-call(s32[2]{0:T(128)S(1)} %pad_add_fusion.3.refs_0_, ...), custom_call_target="tpu_custom_call" | custom-call | flops 5368709120 | tf_op jit(solution)/shard_map/attention_forward/pallas_call | solution.py:353
  13.9 2.9 %collective-permute-start.4 = (bf16[128,1024]{1,0:T(8,128)(2,1)S(1)}, bf16[128,1024]{1,0:T(8,128)(2,1)S(1)}, u32[]{:S(2)}, u32[]{:S(2)}) collective-permute-start(bf16[128,1024]{1,0:T(8,128)(2,1)S(1)} %add_convert_fusion.23), channel_id=1, source_target_pairs={{0,2},{1,3},{2,0},{3,1},{4,6},{5,7},{6,4},{7,5},{8,10},{9,11},{10,... | collective-permute-start | bytes 786440 | tf_op jit(solution)/shard_map/ppermute | solution.py:813
  18.6 5.2 %grad_of_act.1 = (bf16[512,1024]{1,0:T(8,128)(2,1)}, f32[512,1024]{1,0:T(8,128)}) custom-call(s32[2]{0:T(128)S(1)} %pad_add_fusion.3.refs_0_, s32[1,512]{1,0:T(1,128)} %bitcast.41, bf16[512,1024]{1,0:T(8,128)(2,1)} %refs_2_.4, bf16[1024,1024]{1,0:T(8,128)(2,1)} %refs_30_.1, bf16[128,1024]{1,0:T(8,128)(2,1)} %add_convert_fusion.22.refs_4_), custom_call_target="tpu_custom_call" | custom-call | flops 2147483648 | tf_op jit(solution)/shard_map/grad_of_act/pallas_call | solution.py:353
  26.2 7.1 %feed_forward_a.1 = (bf16[256,1024]{1,0:T(8,128)(2,1)}, bf16[256,1024]{1,0:T(8,128)(2,1)}, bf16[256,1024]{1,0:T(8,128)(2,1)}, bf16[128,1024]{1,0:T(8,128)(2,1)}, bf16[128,1024]{1,0:T(8,128)(2,1)}) custom-call(s32[2]{0:T(128)S(1)} %pad_add_fusion.3.refs_0_, s32[1,512]{1,0:T(1,128)} %bitcast.44, bf16[192,512]{1,0:T(8,128)(2,1)} %constant.42.clone.refs_2_.refs_4_.refs_3_, ...), custom_call_target="tpu_custom_call" | custom-call | flops 4294967296 | tf_op jit(solution)/shard_map/feed_forward_a/pallas_call | solution.py:353
  37.6 7.0 %feed_forward_b.1 = (bf16[256,1024]{1,0:T(8,128)(2,1)}, bf16[256,1024]{1,0:T(8,128)(2,1)}, bf16[256,1024]{1,0:T(8,128)(2,1)}, bf16[128,1024]{1,0:T(8,128)(2,1)}, bf16[128,1024]{1,0:T(8,128)(2,1)}) custom-call(s32[2]{0:T(128)S(1)} %pad_add_fusion.3.refs_0_, s32[1,512]{1,0:T(1,128)} %bitcast.45, bf16[192,512]{1,0:T(8,128)(2,1)} %constant.42.clone.refs_2_.refs_4_.refs_3_, ...), custom_call_target="tpu_custom_call" | custom-call | flops 4294967296 | tf_op jit(solution)/shard_map/feed_forward_b/pallas_call | solution.py:353
  48.9 5.3 %collective-permute-done.10 = bf16[128,1024]{1,0:T(8,128)(2,1)S(1)} collective-permute-done((bf16[128,1024]{1,0:T(8,128)(2,1)S(1)}, bf16[128,1024]{1,0:T(8,128)(2,1)S(1)}, u32[]{:S(2)}, u32[]{:S(2)}) %collective-permute-start.10) | collective-permute-done | bytes 262176 | tf_op jit(solution)/shard_map/ppermute | solution.py:813
  54.4 9.9 %feed_weight_grads.1 = (bf16[80,128,128]{2,1,0:T(8,128)(2,1)}, bf16[32,128,128]{2,1,0:T(8,128)(2,1)}, bf16[32,128,128]{2,1,0:T(8,128)(2,1)}) custom-call(s32[2]{0:T(128)S(1)} %pad_add_fusion.3.refs_0_, s32[336]{0:T(512)S(1)} %pad_add_fusion.2.refs_1_, f32[4]{0:T(128)} %pad_maximum_fusion.refs_2_.refs_1_, bf16[256,1024]{1,0:T(8,128)(2,1)} %get-tuple-element.103.refs_3_, ...), custom_call_target="tpu_custom_call" | custom-call | flops 4294967296 | tf_op jit(solution)/shard_map/feed_weight_grads/pallas_call | solution.py:353
  68.3 20.0 %attention_backward.1 = (bf16[64,128,128]{2,1,0:T(8,128)(2,1)S(1)}, bf16[512,1024]{1,0:T(8,128)(2,1)}, bf16[512,1024]{1,0:T(8,128)(2,1)}, bf16[28,128,128]{2,1,0...) custom-call(s32[2]{0:T(128)S(1)} %pad_add_fusion.3.refs_0_, ...), custom_call_target="tpu_custom_call" | custom-call | flops 10737418240 | tf_op jit(solution)/shard_map/attention_backward/pallas_call | solution.py:353
  96.1 8.7 %collective-permute-done.19 = bf16[16,128,128]{2,1,0:T(8,128)(2,1)S(1)} collective-permute-done((bf16[16,128,128]{2,1,0:T(8,128)(2,1)}, bf16[16,128,128]{2,1,0:T(8,128)(2,1)S(1)}, u32[]{:S(2)}, u32[]{:S(2)}) %collective-permute-start.19) | collective-permute-done | bytes 524320 | tf_op jit(solution)/shard_map/ppermute | solution.py:813
  105.7 6.1 %collective-permute-done.18 = bf16[28,128,128]{2,1,0:T(8,128)(2,1)S(1)} collective-permute-done((bf16[28,128,128]{2,1,0:T(8,128)(2,1)}, bf16[28,128,128]{2,1,0:T(8,128)(2,1)S(1)}, u32[]{:S(2)}, u32[]{:S(2)}) %collective-permute-start.18) | collective-permute-done | bytes 917536 | tf_op jit(solution)/shard_map/ppermute | solution.py:813
  113.8 2.0 %collective-permute-done.22 = bf16[16,128,128]{2,1,0:T(8,128)(2,1)S(1)} collective-permute-done((bf16[16,128,128]{2,1,0:T(8,128)(2,1)S(1)}, bf16[16,128,128]{2,1,0:T(8,128)(2,1)S(1)}, u32[]{:S(2)}, u32[]{:S(2)}) %collective-permute-start.22) | collective-permute-done | bytes 524320 | tf_op jit(solution)/shard_map/ppermute | solution.py:813
  118.4 2.6 %collective-permute-start.25 = (bf16[8,128,128]{2,1,0:T(8,128)(2,1)S(1)}, bf16[8,128,128]{2,1,0:T(8,128)(2,1)S(1)}, u32[]{:S(2)}, u32[]{:S(2)}) collective-permute-start(bf16[8,128,128]{2,1,0:T(8,128)(2,1)S(1)} %get-tuple-element.195), channel_id=1, source_target_pairs={{0,16},{4,20},{8,24},{12,28},{16,0},{20,4},{24,8},{28,12},{1,17},{... | collective-permute-start | bytes 786440 | tf_op jit(solution)/shard_map/ppermute | solution.py:813
  121.0 4.9 %collective-permute-done.21 = bf16[20,128,128]{2,1,0:T(8,128)(2,1)S(1)} collective-permute-done((bf16[20,128,128]{2,1,0:T(8,128)(2,1)S(1)}, bf16[20,128,128]{2,1,0:T(8,128)(2,1)S(1)}, u32[]{:S(2)}, u32[]{:S(2)}) %collective-permute-start.21) | collective-permute-done | bytes 655392 | tf_op jit(solution)/shard_map/ppermute | solution.py:813
  127.7 3.5 %collective-permute-done.20 = bf16[14,128,128]{2,1,0:T(8,128)(2,1)S(1)} collective-permute-done((bf16[14,128,128]{2,1,0:T(8,128)(2,1)S(1)}, bf16[14,128,128]{2,1,0:T(8,128)(2,1)S(1)}, u32[]{:S(2)}, u32[]{:S(2)}) %collective-permute-start.20) | collective-permute-done | bytes 458784 | tf_op jit(solution)/shard_map/ppermute | solution.py:813
  133.7 8.6 %collective-permute-done.24 = bf16[10,128,128]{2,1,0:T(8,128)(2,1)S(1)} collective-permute-done((bf16[10,128,128]{2,1,0:T(8,128)(2,1)S(1)}, bf16[10,128,128]{2,1,0:T(8,128)(2,1)S(1)}, u32[]{:S(2)}, u32[]{:S(2)}) %collective-permute-start.24) | collective-permute-done | bytes 327712 | tf_op jit(solution)/shard_map/ppermute | solution.py:813
  146.6 1.9 collective-permute-start.29
  149.6 9.3 %layer_outputs.1 = (f32[512,1024]{1,0:T(8,128)}, f32[512,1024]{1,0:T(8,128)}, f32[8,1024]{1,0:T(8,128)}) custom-call(s32[2]{0:T(128)S(1)} %pad_add_fusion.3.refs_0_, f32[4]{0:T(128)} %pad_maximum_fusion.refs_2_.refs_1_, s32[1,512]{1,0:T(1,128)} %bitcast.47, bf16[192,512]{1,0:T(8,128)(2,1)} %constant.42.clone.refs_2_.refs_4_.refs_3_, ...), custom_call_target="tpu_custom_call" | custom-call | flops 2147483648 | tf_op jit(solution)/shard_map/layer_outputs/pallas_call | solution.py:353
  158.9 4.4 %collective-permute-done.28.refs_9_ = bf16[5,128,128]{2,1,0:T(8,128)(2,1)S(1)} collective-permute-done((bf16[5,128,128]{2,1,0:T(8,128)(2,1)S(1)}, bf16[5,128,128]{2,1,0:T(8,128)(2,1)S(1)}, u32[]{:S(2)}, u32[]{:S(2)}) %collective-permute-start.28) | collective-permute-done | bytes 163872 | tf_op jit(solution)/shard_map/ppermute | solution.py:813
  164.0 5.0 %rotate.1 = (f32[24,128,128]{2,1,0:T(8,128)}, f32[24,128,128]{2,1,0:T(8,128)}, f32[8,128]{1,0:T(8,128)}) custom-call(s32[2]{0:T(128)S(1)} %pad_add_fusion.3.refs_0_, s32[192]{0:T(256)} %compare_select_fusion.1.refs_1_, f32[24,128]{1,0:T(8,128)} %bitcast.31, f32[24,128]{1,0:T(8,128)} %bitcast.33, bf16[8,128,128]{2,1,0:T(8,128)(2,1)} %get-tuple-element.194.refs_4_, ...), custom_call_target="tpu_custom_call" | custom-call | flops 1073741824 | tf_op jit(solution)/shard_map/rotate/pallas_call | solution.py:353
  172.4 2.3 %collective-permute-done.31 = f32[8,128]{1,0:T(8,128)S(1)} collective-permute-done((f32[8,128]{1,0:T(8,128)S(1)}, f32[8,128]{1,0:T(8,128)S(1)}, u32[]{:S(2)}, u32[]{:S(2)}) %collective-permute-start.31) | collective-permute-done | bytes 4128 | tf_op jit(solution)/shard_map/ppermute | solution.py:813
  175.8 2.9 %collective-permute-done.32 = f32[8,1024]{1,0:T(8,128)S(1)} collective-permute-done((f32[8,1024]{1,0:T(8,128)S(1)}, f32[8,1024]{1,0:T(8,128)S(1)}, u32[]{:S(2)}, u32[]{:S(2)}) %collective-permute-start.32) | collective-permute-done | bytes 32800 | tf_op jit(solution)/shard_map/ppermute | solution.py:813
  178.8 3.9 %collective-permute-done.33 = f32[8,1024]{1,0:T(8,128)S(1)} collective-permute-done((f32[8,1024]{1,0:T(8,128)S(1)}, f32[8,1024]{1,0:T(8,128)S(1)}, u32[]{:S(2)}, u32[]{:S(2)}) %collective-permute-start.33) | collective-permute-done | bytes 32800 | tf_op jit(solution)/shard_map/ppermute | solution.py:813
  184.3 3.4 %collective-permute-done.34 = f32[8,1024]{1,0:T(8,128)S(1)} collective-permute-done((f32[8,1024]{1,0:T(8,128)S(1)}, f32[8,1024]{1,0:T(8,128)S(1)}, u32[]{:S(2)}, u32[]{:S(2)}) %collective-permute-start.34) | collective-permute-done | bytes 32800 | tf_op jit(solution)/shard_map/ppermute | solution.py:813
  188.4 9.3 %update.1 = (f32[24,128,128]{2,1,0:T(8,128)}, f32[24,128,128]{2,1,0:T(8,128)}, f32[24,128,128]{2,1,0:T(8,128)}, f32[24,128,128]{2,1,0:T(8,128)}, bf16[24,128,128...) custom-call(s32[2]{0:T(128)S(1)} %pad_add_fusion.3.refs_0_, ...), custom_call_target="tpu_custom_call" | custom-call | flops 1073741824 | tf_op jit(solution)/shard_map/update/pallas_call | solution.py:353
  (155 shorter events, 49.2 us)
Async XLA Ops:
  11.5 5.3 %collective-permute-start.5 = (bf16[128,1024]{1,0:T(8,128)(2,1)}, bf16[128,1024]{1,0:T(8,128)(2,1)S(1)}, u32[]{:S(2)}, u32[]{:S(2)}) collective-permute-start(bf16[128,1024]{1,0:T(8,128)(2,1)} %get-tuple-element.94), channel_id=1, source_target_pairs={{0,1},{1,0},{2,3},{3,2},{4,5},{5,4},{6,7},{7,6},{8,9},{9,8},{10,11... | collective-permute-start | bytes 786440 | tf_op jit(solution)/shard_map/ppermute | solution.py:813
  13.9 9.9 %collective-permute-start.4 = (bf16[128,1024]{1,0:T(8,128)(2,1)S(1)}, bf16[128,1024]{1,0:T(8,128)(2,1)S(1)}, u32[]{:S(2)}, u32[]{:S(2)}) collective-permute-start(bf16[128,1024]{1,0:T(8,128)(2,1)S(1)} %add_convert_fusion.23), channel_id=1, source_target_pairs={{0,2},{1,3},{2,0},{3,1},{4,6},{5,7},{6,4},{7,5},{8,10},{9,11},{10,... | collective-permute-start | bytes 786440 | tf_op jit(solution)/shard_map/ppermute | solution.py:813
  24.1 9.2 %collective-permute-start.7 = (bf16[128,1024]{1,0:T(8,128)(2,1)S(1)}, bf16[128,1024]{1,0:T(8,128)(2,1)S(1)}, u32[]{:S(2)}, u32[]{:S(2)}) collective-permute-start(bf16[128,1024]{1,0:T(8,128)(2,1)S(1)} %copy-done.3), channel_id=1, source_target_pairs={{0,2},{1,3},{2,0},{3,1},{4,6},{5,7},{6,4},{7,5},{8,10},{9,11},{10,... | collective-permute-start | bytes 786440 | tf_op jit(solution)/shard_map/ppermute | solution.py:813
  36.5 8.4 %collective-permute-start.9 = (bf16[128,1024]{1,0:T(8,128)(2,1)}, bf16[128,1024]{1,0:T(8,128)(2,1)S(1)}, u32[]{:S(2)}, u32[]{:S(2)}) collective-permute-start(bf16[128,1024]{1,0:T(8,128)(2,1)} %get-tuple-element.99), channel_id=1, source_target_pairs={{0,1},{1,0},{2,3},{3,2},{4,5},{5,4},{6,7},{7,6},{8,9},{9,8},{10,11... | collective-permute-start | bytes 786440 | tf_op jit(solution)/shard_map/ppermute | solution.py:813
  45.0 9.2 %collective-permute-start.10 = (bf16[128,1024]{1,0:T(8,128)(2,1)S(1)}, bf16[128,1024]{1,0:T(8,128)(2,1)S(1)}, u32[]{:S(2)}, u32[]{:S(2)}) collective-permute-start(bf16[128,1024]{1,0:T(8,128)(2,1)S(1)} %add_convert_fusion.19), channel_id=1, source_target_pairs={{0,2},{1,3},{2,0},{3,1},{4,6},{5,7},{6,4},{7,5},{8,10},{9,11},{10,... | collective-permute-start | bytes 786440 | tf_op jit(solution)/shard_map/ppermute | solution.py:813
  48.0 16.3 %collective-permute-start.13 = (bf16[128,1024]{1,0:T(8,128)(2,1)S(1)}, bf16[128,1024]{1,0:T(8,128)(2,1)S(1)}, u32[]{:S(2)}, u32[]{:S(2)}) collective-permute-start(bf16[128,1024]{1,0:T(8,128)(2,1)S(1)} %add_convert_fusion.18.refs_10_), channel_id=1, source_target_pairs={{0,2},{1,3},{2,0},{3,1},{4,6},{5,7},{6,4},{7,5},{8,10},{9,11},{10,... | collective-permute-start | bytes 786440 | tf_op jit(solution)/shard_map/ppermute | solution.py:813
  54.3 13.2 %collective-permute-start.12 = (bf16[128,1024]{1,0:T(8,128)(2,1)S(1)}, bf16[128,1024]{1,0:T(8,128)(2,1)S(1)}, u32[]{:S(2)}, u32[]{:S(2)}) collective-permute-start(bf16[128,1024]{1,0:T(8,128)(2,1)S(1)} %add_convert_fusion.17.refs_11_.refs_12_), channel_id=1, source_target_pairs={{0,1},{1,0},{2,3},{3,2},{4,5},{5,4},{6,7},{7,6},{8,9},{9,8},{10,11... | collective-permute-start | bytes 786440 | tf_op jit(solution)/shard_map/ppermute | solution.py:813
  65.9 25.5 %collective-permute-start.16 = (bf16[32,128,128]{2,1,0:T(8,128)(2,1)}, bf16[32,128,128]{2,1,0:T(8,128)(2,1)}, u32[]{:S(2)}, u32[]{:S(2)}) collective-permute-start(bf16[32,128,128]{2,1,0:T(8,128)(2,1)} %get-tuple-element.120), channel_id=1, source_target_pairs={{0,4},{4,0},{8,12},{12,8},{16,20},{20,16},{24,28},{28,24},{1,5},{5... | collective-permute-start | bytes 3145736 | tf_op jit(solution)/shard_map/ppermute | solution.py:813
  88.3 7.8 %collective-permute-start.15 = (bf16[512,1024]{1,0:T(8,128)(2,1)}, bf16[512,1024]{1,0:T(8,128)(2,1)S(1)}, u32[]{:S(2)}, u32[]{:S(2)}) collective-permute-start(bf16[512,1024]{1,0:T(8,128)(2,1)} %get-tuple-element.119), channel_id=1, source_target_pairs={{0,1},{1,0},{2,3},{3,2},{4,5},{5,4},{6,7},{7,6},{8,9},{9,8},{10,11... | collective-permute-start | bytes 3145736 | tf_op jit(solution)/shard_map/ppermute | solution.py:813
  88.4 23.4 %collective-permute-start.18 = (bf16[28,128,128]{2,1,0:T(8,128)(2,1)}, bf16[28,128,128]{2,1,0:T(8,128)(2,1)S(1)}, u32[]{:S(2)}, u32[]{:S(2)}) collective-permute-start(bf16[28,128,128]{2,1,0:T(8,128)(2,1)} %get-tuple-element.125), channel_id=1, source_target_pairs={{0,4},{4,0},{8,12},{12,8},{16,20},{20,16},{24,28},{28,24},{1,5},{5... | collective-permute-start | bytes 2752520 | tf_op jit(solution)/shard_map/ppermute | solution.py:813
  89.8 15.0 %collective-permute-start.19 = (bf16[16,128,128]{2,1,0:T(8,128)(2,1)}, bf16[16,128,128]{2,1,0:T(8,128)(2,1)S(1)}, u32[]{:S(2)}, u32[]{:S(2)}) collective-permute-start(bf16[16,128,128]{2,1,0:T(8,128)(2,1)} %get-tuple-element.126), channel_id=1, source_target_pairs={{0,8},{4,12},{8,0},{12,4},{16,24},{20,28},{24,16},{28,20},{1,9},{5... | collective-permute-start | bytes 1572872 | tf_op jit(solution)/shard_map/ppermute | solution.py:813
  93.0 22.8 %collective-permute-start.22 = (bf16[16,128,128]{2,1,0:T(8,128)(2,1)S(1)}, bf16[16,128,128]{2,1,0:T(8,128)(2,1)S(1)}, u32[]{:S(2)}, u32[]{:S(2)}) collective-permute-start(bf16[16,128,128]{2,1,0:T(8,128)(2,1)S(1)} %get-tuple-element.189), channel_id=1, source_target_pairs={{0,8},{4,12},{8,0},{12,4},{16,24},{20,28},{24,16},{28,20},{1,9},{5... | collective-permute-start | bytes 1572872 | tf_op jit(solution)/shard_map/ppermute | solution.py:813
  94.6 31.3 %collective-permute-start.21 = (bf16[20,128,128]{2,1,0:T(8,128)(2,1)S(1)}, bf16[20,128,128]{2,1,0:T(8,128)(2,1)S(1)}, u32[]{:S(2)}, u32[]{:S(2)}) collective-permute-start(bf16[20,128,128]{2,1,0:T(8,128)(2,1)S(1)} %copy-done.17), channel_id=1, source_target_pairs={{0,4},{4,0},{8,12},{12,8},{16,20},{20,16},{24,28},{28,24},{1,5},{5... | collective-permute-start | bytes 1966088 | tf_op jit(solution)/shard_map/ppermute | solution.py:813
  105.0 28.0 %collective-permute-start.26 = (bf16[8,128,128]{2,1,0:T(8,128)(2,1)S(1)}, bf16[8,128,128]{2,1,0:T(8,128)(2,1)S(1)}, u32[]{:S(2)}, u32[]{:S(2)}) collective-permute-start(bf16[8,128,128]{2,1,0:T(8,128)(2,1)S(1)} %get-tuple-element.197), channel_id=1, source_target_pairs={{0,4},{4,0},{8,12},{12,8},{16,20},{20,16},{24,28},{28,24},{1,5},{5... | collective-permute-start | bytes 786440 | tf_op jit(solution)/shard_map/ppermute | solution.py:813
  112.2 19.1 %collective-permute-start.20 = (bf16[14,128,128]{2,1,0:T(8,128)(2,1)S(1)}, bf16[14,128,128]{2,1,0:T(8,128)(2,1)S(1)}, u32[]{:S(2)}, u32[]{:S(2)}) collective-permute-start(bf16[14,128,128]{2,1,0:T(8,128)(2,1)S(1)} %get-tuple-element.190), channel_id=1, source_target_pairs={{0,8},{4,12},{8,0},{12,4},{16,24},{20,28},{24,16},{28,20},{1,9},{5... | collective-permute-start | bytes 1376264 | tf_op jit(solution)/shard_map/ppermute | solution.py:813
  116.2 27.6 %collective-permute-start.17 = (bf16[512,1024]{1,0:T(8,128)(2,1)S(1)}, bf16[512,1024]{1,0:T(8,128)(2,1)S(1)}, u32[]{:S(2)}, u32[]{:S(2)}) collective-permute-start(bf16[512,1024]{1,0:T(8,128)(2,1)S(1)} %add_convert_fusion.5), channel_id=1, source_target_pairs={{0,2},{1,3},{2,0},{3,1},{4,6},{5,7},{6,4},{7,5},{8,10},{9,11},{10,... | collective-permute-start | bytes 3145736 | tf_op jit(solution)/shard_map/ppermute | solution.py:813
  118.4 15.3 %collective-permute-start.25 = (bf16[8,128,128]{2,1,0:T(8,128)(2,1)S(1)}, bf16[8,128,128]{2,1,0:T(8,128)(2,1)S(1)}, u32[]{:S(2)}, u32[]{:S(2)}) collective-permute-start(bf16[8,128,128]{2,1,0:T(8,128)(2,1)S(1)} %get-tuple-element.195), channel_id=1, source_target_pairs={{0,16},{4,20},{8,24},{12,28},{16,0},{20,4},{24,8},{28,12},{1,17},{... | collective-permute-start | bytes 786440 | tf_op jit(solution)/shard_map/ppermute | solution.py:813
  126.1 16.2 %collective-permute-start.24 = (bf16[10,128,128]{2,1,0:T(8,128)(2,1)S(1)}, bf16[10,128,128]{2,1,0:T(8,128)(2,1)S(1)}, u32[]{:S(2)}, u32[]{:S(2)}) collective-permute-start(bf16[10,128,128]{2,1,0:T(8,128)(2,1)S(1)} %get-tuple-element.193), channel_id=1, source_target_pairs={{0,8},{4,12},{8,0},{12,4},{16,24},{20,28},{24,16},{28,20},{1,9},{5... | collective-permute-start | bytes 983048 | tf_op jit(solution)/shard_map/ppermute | solution.py:813
  132.1 11.0 %collective-permute-start.23 = (bf16[7,128,128]{2,1,0:T(8,128)(2,1)S(1)}, bf16[7,128,128]{2,1,0:T(8,128)(2,1)S(1)}, u32[]{:S(2)}, u32[]{:S(2)}) collective-permute-start(bf16[7,128,128]{2,1,0:T(8,128)(2,1)S(1)} %get-tuple-element.199), channel_id=1, source_target_pairs={{0,16},{4,20},{8,24},{12,28},{16,0},{20,4},{24,8},{28,12},{1,17},{... | collective-permute-start | bytes 688136 | tf_op jit(solution)/shard_map/ppermute | solution.py:813
  144.2 5.4 %collective-permute-start.27 = (bf16[512,1024]{1,0:T(8,128)(2,1)S(1)}, bf16[512,1024]{1,0:T(8,128)(2,1)}, u32[]{:S(2)}, u32[]{:S(2)}) collective-permute-start(bf16[512,1024]{1,0:T(8,128)(2,1)S(1)} %add_convert_fusion.4.refs_10_), channel_id=1, source_target_pairs={{0,1},{1,0},{2,3},{3,2},{4,5},{5,4},{6,7},{7,6},{8,9},{9,8},{10,11... | collective-permute-start | bytes 3145736 | tf_op jit(solution)/shard_map/ppermute | solution.py:813
  146.6 16.7 %collective-permute-start.29 = (bf16[4,128,128]{2,1,0:T(8,128)(2,1)S(1)}, bf16[4,128,128]{2,1,0:T(8,128)(2,1)S(1)}, u32[]{:S(2)}, u32[]{:S(2)}) collective-permute-start(bf16[4,128,128]{2,1,0:T(8,128)(2,1)S(1)} %get-tuple-element.203), channel_id=1, source_target_pairs={{0,16},{4,20},{8,24},{12,28},{16,0},{20,4},{24,8},{28,12},{1,17},{... | collective-permute-start | bytes 393224 | tf_op jit(solution)/shard_map/ppermute | solution.py:813
  148.5 14.7 %collective-permute-start.28 = (bf16[5,128,128]{2,1,0:T(8,128)(2,1)S(1)}, bf16[5,128,128]{2,1,0:T(8,128)(2,1)S(1)}, u32[]{:S(2)}, u32[]{:S(2)}) collective-permute-start(bf16[5,128,128]{2,1,0:T(8,128)(2,1)S(1)} %get-tuple-element.201), channel_id=1, source_target_pairs={{0,16},{4,20},{8,24},{12,28},{16,0},{20,4},{24,8},{28,12},{1,17},{... | collective-permute-start | bytes 491528 | tf_op jit(solution)/shard_map/ppermute | solution.py:813
  174.8 4.0 %collective-permute-start.32 = (f32[8,1024]{1,0:T(8,128)S(1)}, f32[8,1024]{1,0:T(8,128)S(1)}, u32[]{:S(2)}, u32[]{:S(2)}) collective-permute-start(f32[8,1024]{1,0:T(8,128)S(1)} %pad_add_fusion), channel_id=1, source_target_pairs={{0,4},{4,0},{8,12},{12,8},{16,20},{20,16},{24,28},{28,24},{1,5},{5... | collective-permute-start | bytes 98312 | tf_op jit(solution)/shard_map/ppermute | solution.py:813
  182.7 5.0 %collective-permute-start.34 = (f32[8,1024]{1,0:T(8,128)S(1)}, f32[8,1024]{1,0:T(8,128)S(1)}, u32[]{:S(2)}, u32[]{:S(2)}) collective-permute-start(f32[8,1024]{1,0:T(8,128)S(1)} %add.162), channel_id=1, source_target_pairs={{0,16},{4,20},{8,24},{12,28},{16,0},{20,4},{24,8},{28,12},{1,17},{... | collective-permute-start | bytes 98312 | tf_op jit(solution)/shard_map/ppermute | solution.py:813
  (34 other events, 216.5 us)
where the time goes:
time: 199 us
  Pallas kernels  83.1 us (42%)
  waiting for transfers between devices  57.6 us (29%)
  starting transfers between devices  32.5 us (16%)
  other arithmetic  15.6 us (8%)
  local copies, waits for them, and re-layouts  6.28 us (3%)
  between operations  3.81 us (2%)
    pallas_call x9, Pallas kernels, call(): pl.pallas_call(body, name=name, out_shape=results, in_specs=[pl.BlockSpec...  83.1 us
    ppermute x32, waiting for transfers between devices, swap(): return lax.ppermute(value, axis, [(i, i ^ bit) for i in range(count)])  57.6 us
    ppermute x32, starting transfers between devices, swap(): return lax.ppermute(value, axis, [(i, i ^ bit) for i in range(count)])  32.5 us
    convert_element_type x18, other arithmetic, plus(): return (left.astype(F32) + right.astype(F32)).astype(BF16)  11.3 us
  transfers between devices with their start and end apart: 32, of which 14 were waited for; matrix products, arithmetic and copies ran while one was open for 8% of the time, Pallas kernels for 29%

commit v1 on v0

--- a/solution.py
+++ b/solution.py
@@ -350,12 +350,13 @@
             copy.wait()
 
     hbm = pl.BlockSpec(memory_space=pltpu.HBM)
+    scalar = pl.BlockSpec(memory_space=pltpu.SMEM)
     return pl.pallas_call(
         body,
         name=name,
         out_shape=results,
         in_specs=[pl.BlockSpec(memory_space=pltpu.SMEM)] * n_scalar + [hbm] * n_in,
-        out_specs=[hbm] * n_out,
+        out_specs=[scalar if r.shape == (1, 1) else hbm for r in results],
         scratch_shapes=[pltpu.VMEM(shape, kind) for shape, kind in shapes]
         + [pltpu.VMEM(shape, kind) for shape, kind, *_ in outs]
         + [pltpu.SemaphoreType.DMA((max(n_in, 1),)), pltpu.SemaphoreType.DMA((len(outs), SEMS))]
@@ -446,12 +447,12 @@
     part.send()
 
 
-def store_blocks(nat_ref, base, left, right_ref, weight):
+def store_blocks(nat_ref, base, left, right_ref, weight, unroll=False):
     width = right_ref.shape[1]
     across = width // BLK
     wide = 256
 
-    @pl.loop(0, width // wide)
+    @pl.loop(0, width // wide, unroll=unroll)
     def _(step):
         cols = pl.ds(pl.multiple_of(step * wide, wide), wide)
         grad = (dot_tn(left, right_ref[:, cols]) * weight).astype(BF16)
@@ -488,8 +489,8 @@
     second, gpre, act, gout = loads
     rest = stores[0]
     weight = scal_ref[0]
-    store_blocks(nat_ref, 0, second()[...], gpre(), weight)
-    store_blocks(nat_ref, 64, act()[...], gout(), weight)
+    store_blocks(nat_ref, 0, second()[...], gpre(), weight, True)
+    store_blocks(nat_ref, 64, act()[...], gout(), weight, True)
 
     def block_at(block):
         return nat_ref[jnp.maximum(block - late_count, 0)]
@@ -792,8 +793,7 @@
         out_copy.ref[rows] = fresh.astype(BF16)
         for out in (out_grad, out_first, out_second, out_master, out_copy):
             out.send(rows)
-    clip_out.ref[...] = jnp.broadcast_to(clip_norm, clip_out.ref.shape)
-    clip_out.send()
+    clip_out.target[0, 0] = clip_norm[0, 0]
     clipped = norm_grad * clip[:, 0:1]
     first = beta_one * norm_first()[...] + (1.0 - beta_one) * clipped
     second = beta_two * norm_second()[...] + (1.0 - beta_two) * clipped * clipped
@@ -843,8 +843,7 @@
     if slots >= 8:
         last = slots // 4
         head = (slots - last + 2) // 2
-        crossed = (bits[1], bits[0]) + bits[2:]
-        return ((head, bits), (slots - last - head, bits), (last, crossed))
+        return ((head, bits), (slots - last - head, bits), (last, (bits[1], bits[0]) + bits[2:]))
     return ((1, bits),) * slots if slots <= 3 else ((slots - slots // 2, bits), (slots // 2, bits))
 
 
@@ -1013,7 +1012,6 @@
     second_b, act_b, gpre_b, keep_b, send_b = feed(half, "feed_forward_b", attn_b, keep_a)
     near_a = plus(keep_a, swap(send_a, "mp", 1))
     near_b = plus(keep_b, swap(send_b, "mp", 1))
-    far_a = mp_far(near_a, near_b)
     chunk_e = [((n_dp // 2 * early_slots, BLK, BLK), BF16)] * 2 if early_slots else []
     count = rest_count(blocks, late_count, n_dp, slots, early_slots)
     rest, *chunk_e = call(
@@ -1026,7 +1024,8 @@
         flops=4 * unit,
         after=near_b,
     )
-    far_b = mp_far(near_b, rest)
+    far_a = mp_far(near_a, rest)
+    far_b = mp_far(near_b, far_a)
     sum_a = Pair(far_a, swap(far_a, "mp", 1))
     sum_b = Pair(far_b, swap(far_b, "mp", 1))
     got_e = swap(chunk_e[1], "dp", 1) if early_slots else None
@@ -1131,25 +1130,7 @@
         last.append(outputs[2])
         return outputs
 
-    plan = ["near", "far", "finish"]
-    if early_slots and stages == 3:
-        plan = ["near",(3,0),(1,0),(0,1),(2,0),(1,1),(3,1),(0,2),(2,1),(1,2),"far","finish"]
-    plan += [(i, d - i) for d in range(len(state) + stages) for i in range(len(state))]
-    for entry in plan:
-        if entry == "near":
-            near = plus(keep, in_turn(swap(send, "mp", 1)))
-        elif entry == "far":
-            bit = 2
-            while bit < lax.axis_size("mp"):
-                near = plus(near, in_turn(swap(near, "mp", bit)))
-                bit *= 2
-            both = Pair(near, swap(near, "mp", 1))
-        elif entry == "finish":
-            out, input_grad, sums = finish(both)
-        elif level[entry[0]] == entry[1] < stages:
-            halve(entry[0])
-    pending = [array for pair in state for array in pair]
-
+    overflow, early_done = [], []
     if early_slots:
         shape = (n_dp // 2 * early_slots, BLK, BLK)
 
@@ -1174,9 +1155,31 @@
             zero = jnp.zeros((early_slots, BLK, BLK), BF16)
             return (zero, zero)
 
-        pending += list(lax.cond(short, exchange, nothing, late))
-        counts.append(early_slots)
-
+        overflow = list(lax.cond(short, exchange, nothing, late))
+        early_done = [overflow[0], place]
+
+    plan = ["near", "far", "finish"]
+    if early_slots and stages == 3:
+        plan = ["near",(3,0),(1,0),(0,1),(2,0),(1,1),(3,1),(0,2),(2,1),(1,2),"far","finish"]
+    plan += [(i, d - i) for d in range(len(state) + stages) for i in range(len(state))]
+    for entry in plan:
+        if entry == "near":
+            near = plus(keep, in_turn(swap(send, "mp", 1)))
+            last += early_done
+        elif entry == "far":
+            bit = 2
+            while bit < lax.axis_size("mp"):
+                near = plus(near, in_turn(swap(near, "mp", bit)))
+                bit *= 2
+            both = Pair(near, swap(near, "mp", 1))
+        elif entry == "finish":
+            out, input_grad, sums = finish(both)
+        elif level[entry[0]] == entry[1] < stages:
+            halve(entry[0])
+    pending = [array for pair in state for array in pair]
+
+    pending += overflow
+    counts += [early_slots] if early_slots else []
     left = left_vector.reshape(slots, BLK)
     right = right_vector.reshape(slots, BLK)
     block_f32 = ((slots, BLK, BLK), F32)
@@ -1222,7 +1225,7 @@
             ((2, 4, D), F32),
             ((4, D), F32),
             ((4, D), F32),
-            ((8, BLK), F32),
+            ((1, 1), F32),
         ],
         flops=unit,
     )
@@ -1238,7 +1241,7 @@
         new[5],
         new[6],
         new[7],
-        new[8][0, 0],
+        new[8].reshape(()),
     )
 
 

time: 199 us -> 191 us (0.960)
  waiting for transfers between devices: 57.6 us -> 46.5 us
  other arithmetic: 15.6 us -> 20.2 us
    ppermute x32, waiting for transfers between devices: 57.6 us -> 46.5 us  [swap(): return lax.ppermute(value, axis, [(i, i ^ bit) for i in range(count)])]
    convert_element_type x18, other arithmetic: 11.3 us -> 15.9 us  [plus(): return (left.astype(F32) + right.astype(F32)).astype(BF16)]
  transfers between devices with their start and end apart: 32 -> 32, of which waited for: 14 -> 15; matrix products, arithmetic and copies ran while one was open for 8% -> 11% of each run, Pallas kernels for 29% -> 30%
where the time goes in v1:
time: 191 us
  Pallas kernels  81.9 us (43%)
  waiting for transfers between devices  46.5 us (24%)
  starting transfers between devices  32.3 us (17%)
  other arithmetic  20.2 us (11%)
  local copies, waits for them, and re-layouts  5.88 us (3%)
  between operations  3.96 us (2%)
    pallas_call x9, Pallas kernels, call(): pl.pallas_call(body, name=name, out_shape=results, in_specs=[pl.BlockSpec...  81.9 us
    ppermute x32, waiting for transfers between devices, swap(): return lax.ppermute(value, axis, [(i, i ^ bit) for i in range(count)])  46.5 us
    ppermute x32, starting transfers between devices, swap(): return lax.ppermute(value, axis, [(i, i ^ bit) for i in range(count)])  32.3 us
    convert_element_type x18, other arithmetic, plus(): return (left.astype(F32) + right.astype(F32)).astype(BF16)  15.9 us
    unnamed x58, local copies, waits for them, and re-layouts  3.95 us
  transfers between devices with their start and end apart: 32, of which 15 were waited for; matrix products, arithmetic and copies ran while one was open for 11% of the time, Pallas kernels for 30%

profile of v1, /device:TPU:0, one launch (start us, length us, event | category | flops | bytes accessed | tf_op | source)
XLA Modules:
  0.0 190.7 jit_solution(15517273112205750618)
XLA Ops:
  0.7 10.3 %attention_forward.1 = (bf16[512,1024]{1,0:T(8,128)(2,1)}, bf16[512,256]{1,0:T(8,128)(2,1)}, bf16[512,256]{1,0:T(8,128)(2,1)}, bf16[512,256]{1,0:T(8,128)(2,1)},...) custom-call(s32[2]{0:T(128)S(1)} %pad_add_fusion.3.refs_0_, ...), custom_call_target="tpu_custom_call" | custom-call | flops 5368709120 | tf_op jit(solution)/shard_map/attention_forward/pallas_call | solution.py:354
  13.9 2.9 %collective-permute-start.4 = (bf16[128,1024]{1,0:T(8,128)(2,1)S(1)}, bf16[128,1024]{1,0:T(8,128)(2,1)S(1)}, u32[]{:S(2)}, u32[]{:S(2)}) collective-permute-start(bf16[128,1024]{1,0:T(8,128)(2,1)S(1)} %add_convert_fusion.23), channel_id=1, source_target_pairs={{0,2},{1,3},{2,0},{3,1},{4,6},{5,7},{6,4},{7,5},{8,10},{9,11},{10,... | collective-permute-start | bytes 786440 | tf_op jit(solution)/shard_map/ppermute | solution.py:813
  18.6 5.2 %grad_of_act.1 = (bf16[512,1024]{1,0:T(8,128)(2,1)}, f32[512,1024]{1,0:T(8,128)}) custom-call(s32[2]{0:T(128)S(1)} %pad_add_fusion.3.refs_0_, s32[1,512]{1,0:T(1,128)} %bitcast.41, bf16[512,1024]{1,0:T(8,128)(2,1)} %refs_2_.4, bf16[1024,1024]{1,0:T(8,128)(2,1)} %refs_30_.1, bf16[128,1024]{1,0:T(8,128)(2,1)} %add_convert_fusion.22.refs_4_), custom_call_target="tpu_custom_call" | custom-call | flops 2147483648 | tf_op jit(solution)/shard_map/grad_of_act/pallas_call | solution.py:354
  26.2 7.1 %feed_forward_a.1 = (bf16[256,1024]{1,0:T(8,128)(2,1)}, bf16[256,1024]{1,0:T(8,128)(2,1)}, bf16[256,1024]{1,0:T(8,128)(2,1)}, bf16[128,1024]{1,0:T(8,128)(2,1)}, bf16[128,1024]{1,0:T(8,128)(2,1)}) custom-call(s32[2]{0:T(128)S(1)} %pad_add_fusion.3.refs_0_, s32[1,512]{1,0:T(1,128)} %bitcast.44, bf16[192,512]{1,0:T(8,128)(2,1)} %constant.42.clone.refs_2_.refs_4_.refs_3_, ...), custom_call_target="tpu_custom_call" | custom-call | flops 4294967296 | tf_op jit(solution)/shard_map/feed_forward_a/pallas_call | solution.py:354
  37.6 7.0 %feed_forward_b.1 = (bf16[256,1024]{1,0:T(8,128)(2,1)}, bf16[256,1024]{1,0:T(8,128)(2,1)}, bf16[256,1024]{1,0:T(8,128)(2,1)}, bf16[128,1024]{1,0:T(8,128)(2,1)}, bf16[128,1024]{1,0:T(8,128)(2,1)}) custom-call(s32[2]{0:T(128)S(1)} %pad_add_fusion.3.refs_0_, s32[1,512]{1,0:T(1,128)} %bitcast.45, bf16[192,512]{1,0:T(8,128)(2,1)} %constant.42.clone.refs_2_.refs_4_.refs_3_, ...), custom_call_target="tpu_custom_call" | custom-call | flops 4294967296 | tf_op jit(solution)/shard_map/feed_forward_b/pallas_call | solution.py:354
  48.9 8.4 %feed_weight_grads.1 = (bf16[80,128,128]{2,1,0:T(8,128)(2,1)}, bf16[32,128,128]{2,1,0:T(8,128)(2,1)}, bf16[32,128,128]{2,1,0:T(8,128)(2,1)}) custom-call(s32[2]{0:T(128)S(1)} %pad_add_fusion.3.refs_0_, s32[336]{0:T(512)S(1)} %pad_add_fusion.2.refs_1_, f32[4]{0:T(128)} %pad_maximum_fusion.refs_2_.refs_1_, bf16[256,1024]{1,0:T(8,128)(2,1)} %get-tuple-element.100.refs_3_, ...), custom_call_target="tpu_custom_call" | custom-call | flops 4294967296 | tf_op jit(solution)/shard_map/feed_weight_grads/pallas_call | solution.py:354
  57.5 2.3 %collective-permute-done.13 = bf16[128,1024]{1,0:T(8,128)(2,1)S(1)} collective-permute-done((bf16[128,1024]{1,0:T(8,128)(2,1)S(1)}, bf16[128,1024]{1,0:T(8,128)(2,1)S(1)}, u32[]{:S(2)}, u32[]{:S(2)}) %collective-permute-start.13) | collective-permute-done | bytes 262176 | tf_op jit(solution)/shard_map/ppermute | solution.py:813
  63.3 19.9 %attention_backward.1 = (bf16[64,128,128]{2,1,0:T(8,128)(2,1)S(1)}, bf16[512,1024]{1,0:T(8,128)(2,1)}, bf16[512,1024]{1,0:T(8,128)(2,1)}, bf16[28,128,128]{2,1,0...) custom-call(s32[2]{0:T(128)S(1)} %pad_add_fusion.3.refs_0_, ...), custom_call_target="tpu_custom_call" | custom-call | flops 10737418240 | tf_op jit(solution)/shard_map/attention_backward/pallas_call | solution.py:354
  87.1 2.7 %add_convert_fusion.6 = (bf16[16,128,128]{2,1,0:T(8,128)(2,1)S(1)}, bf16[16,128,128]{2,1,0:T(8,128)(2,1)}) fusion(bf16[32,128,128]{2,1,0:T(8,128)(2,1)} %collective-permute-done.16, bf16[32,128,128]{2,1,0:T(8,128)(2,1)} %get-tuple-element.122), kind=kLoop, calls=%fused_computation.6 | loop fusion | flops 2097152 | bytes 3145728 | tf_op jit(solution)/shard_map/convert_element_type | solution.py:817
  95.0 4.8 %collective-permute-done.19 = bf16[16,128,128]{2,1,0:T(8,128)(2,1)} collective-permute-done((bf16[16,128,128]{2,1,0:T(8,128)(2,1)}, bf16[16,128,128]{2,1,0:T(8,128)(2,1)}, u32[]{:S(2)}, u32[]{:S(2)}) %collective-permute-start.19) | collective-permute-done | bytes 524320 | tf_op jit(solution)/shard_map/ppermute | solution.py:813
  102.0 4.8 %collective-permute-done.18 = bf16[28,128,128]{2,1,0:T(8,128)(2,1)S(1)} collective-permute-done((bf16[28,128,128]{2,1,0:T(8,128)(2,1)}, bf16[28,128,128]{2,1,0:T(8,128)(2,1)S(1)}, u32[]{:S(2)}, u32[]{:S(2)}) %collective-permute-start.18) | collective-permute-done | bytes 917536 | tf_op jit(solution)/shard_map/ppermute | solution.py:813
  108.8 2.3 %collective-permute-done.22 = bf16[16,128,128]{2,1,0:T(8,128)(2,1)} collective-permute-done((bf16[16,128,128]{2,1,0:T(8,128)(2,1)}, bf16[16,128,128]{2,1,0:T(8,128)(2,1)}, u32[]{:S(2)}, u32[]{:S(2)}) %collective-permute-start.22) | collective-permute-done | bytes 524320 | tf_op jit(solution)/shard_map/ppermute | solution.py:813
  116.0 2.6 %collective-permute-start.25 = (bf16[8,128,128]{2,1,0:T(8,128)(2,1)S(1)}, bf16[8,128,128]{2,1,0:T(8,128)(2,1)S(1)}, u32[]{:S(2)}, u32[]{:S(2)}) collective-permute-start(bf16[8,128,128]{2,1,0:T(8,128)(2,1)S(1)} %get-tuple-element.195), channel_id=1, source_target_pairs={{0,16},{4,20},{8,24},{12,28},{16,0},{20,4},{24,8},{28,12},{1,17},{... | collective-permute-start | bytes 786440 | tf_op jit(solution)/shard_map/ppermute | solution.py:813
  122.6 2.5 %collective-permute-done.20 = bf16[14,128,128]{2,1,0:T(8,128)(2,1)S(1)} collective-permute-done((bf16[14,128,128]{2,1,0:T(8,128)(2,1)S(1)}, bf16[14,128,128]{2,1,0:T(8,128)(2,1)S(1)}, u32[]{:S(2)}, u32[]{:S(2)}) %collective-permute-start.20) | collective-permute-done | bytes 458784 | tf_op jit(solution)/shard_map/ppermute | solution.py:813
  126.8 2.8 %collective-permute-done.25.refs_5_ = bf16[8,128,128]{2,1,0:T(8,128)(2,1)S(1)} collective-permute-done((bf16[8,128,128]{2,1,0:T(8,128)(2,1)S(1)}, bf16[8,128,128]{2,1,0:T(8,128)(2,1)S(1)}, u32[]{:S(2)}, u32[]{:S(2)}) %collective-permute-start.25) | collective-permute-done | bytes 262176 | tf_op jit(solution)/shard_map/ppermute | solution.py:813
  129.6 7.9 %collective-permute-done.24 = bf16[10,128,128]{2,1,0:T(8,128)(2,1)S(1)} collective-permute-done((bf16[10,128,128]{2,1,0:T(8,128)(2,1)S(1)}, bf16[10,128,128]{2,1,0:T(8,128)(2,1)S(1)}, u32[]{:S(2)}, u32[]{:S(2)}) %collective-permute-start.24) | collective-permute-done | bytes 327712 | tf_op jit(solution)/shard_map/ppermute | solution.py:813
  142.7 9.2 %layer_outputs.1 = (f32[512,1024]{1,0:T(8,128)}, f32[512,1024]{1,0:T(8,128)}, f32[8,1024]{1,0:T(8,128)}) custom-call(s32[2]{0:T(128)S(1)} %copy-done.18, f32[4]{0:T(128)} %pad_maximum_fusion.refs_2_.refs_1_, s32[1,512]{1,0:T(1,128)} %bitcast.47, bf16[192,512]{1,0:T(8,128)(2,1)} %constant.42.clone.refs_2_.refs_4_.refs_3_, bf16[512,1024]{1,0:T(8,128)(2,1)} %refs_4_.3, ...), custom_call_target="tpu_custom_call" | custom-call | flops 2147483648 | tf_op jit(solution)/shard_map/layer_outputs/pallas_call | solution.py:354
  152.0 3.4 %collective-permute-done.28.refs_9_ = bf16[5,128,128]{2,1,0:T(8,128)(2,1)S(1)} collective-permute-done((bf16[5,128,128]{2,1,0:T(8,128)(2,1)S(1)}, bf16[5,128,128]{2,1,0:T(8,128)(2,1)S(1)}, u32[]{:S(2)}, u32[]{:S(2)}) %collective-permute-start.28) | collective-permute-done | bytes 163872 | tf_op jit(solution)/shard_map/ppermute | solution.py:813
  156.1 5.0 %rotate.1 = (f32[24,128,128]{2,1,0:T(8,128)}, f32[24,128,128]{2,1,0:T(8,128)}, f32[8,128]{1,0:T(8,128)}) custom-call(s32[2]{0:T(128)S(1)} %copy-done.18, s32[192]{0:T(256)} %compare_select_fusion.1.refs_1_, f32[24,128]{1,0:T(8,128)} %bitcast.31, f32[24,128]{1,0:T(8,128)} %bitcast.33, bf16[8,128,128]{2,1,0:T(8,128)(2,1)} %get-tuple-element.194.refs_4_, ...), custom_call_target="tpu_custom_call" | custom-call | flops 1073741824 | tf_op jit(solution)/shard_map/rotate/pallas_call | solution.py:354
  164.6 2.3 %collective-permute-done.31 = f32[8,128]{1,0:T(8,128)S(1)} collective-permute-done((f32[8,128]{1,0:T(8,128)S(1)}, f32[8,128]{1,0:T(8,128)S(1)}, u32[]{:S(2)}, u32[]{:S(2)}) %collective-permute-start.31) | collective-permute-done | bytes 4128 | tf_op jit(solution)/shard_map/ppermute | solution.py:813
  168.5 2.4 %collective-permute-done.32 = f32[8,1024]{1,0:T(8,128)S(1)} collective-permute-done((f32[8,1024]{1,0:T(8,128)S(1)}, f32[8,1024]{1,0:T(8,128)S(1)}, u32[]{:S(2)}, u32[]{:S(2)}) %collective-permute-start.32) | collective-permute-done | bytes 32800 | tf_op jit(solution)/shard_map/ppermute | solution.py:813
  171.2 3.7 %collective-permute-done.33 = f32[8,1024]{1,0:T(8,128)S(1)} collective-permute-done((f32[8,1024]{1,0:T(8,128)S(1)}, f32[8,1024]{1,0:T(8,128)S(1)}, u32[]{:S(2)}, u32[]{:S(2)}) %collective-permute-start.33) | collective-permute-done | bytes 32800 | tf_op jit(solution)/shard_map/ppermute | solution.py:813
  176.6 3.5 %collective-permute-done.34 = f32[8,1024]{1,0:T(8,128)S(1)} collective-permute-done((f32[8,1024]{1,0:T(8,128)S(1)}, f32[8,1024]{1,0:T(8,128)S(1)}, u32[]{:S(2)}, u32[]{:S(2)}) %collective-permute-start.34) | collective-permute-done | bytes 32800 | tf_op jit(solution)/shard_map/ppermute | solution.py:813
  180.7 9.8 %update.1 = (f32[24,128,128]{2,1,0:T(8,128)}, f32[24,128,128]{2,1,0:T(8,128)}, f32[24,128,128]{2,1,0:T(8,128)}, f32[24,128,128]{2,1,0:T(8,128)}, bf16[24,128,128...) custom-call(s32[2]{0:T(128)S(1)} %copy-done.18, ...), custom_call_target="tpu_custom_call" | custom-call | flops 1073741824 | tf_op jit(solution)/shard_map/update/pallas_call | solution.py:354
  (160 shorter events, 54.6 us)
Async XLA Ops:
  11.5 5.3 %collective-permute-start.5 = (bf16[128,1024]{1,0:T(8,128)(2,1)}, bf16[128,1024]{1,0:T(8,128)(2,1)S(1)}, u32[]{:S(2)}, u32[]{:S(2)}) collective-permute-start(bf16[128,1024]{1,0:T(8,128)(2,1)} %get-tuple-element.94), channel_id=1, source_target_pairs={{0,1},{1,0},{2,3},{3,2},{4,5},{5,4},{6,7},{7,6},{8,9},{9,8},{10,11... | collective-permute-start | bytes 786440 | tf_op jit(solution)/shard_map/ppermute | solution.py:813
  13.9 9.8 %collective-permute-start.4 = (bf16[128,1024]{1,0:T(8,128)(2,1)S(1)}, bf16[128,1024]{1,0:T(8,128)(2,1)S(1)}, u32[]{:S(2)}, u32[]{:S(2)}) collective-permute-start(bf16[128,1024]{1,0:T(8,128)(2,1)S(1)} %add_convert_fusion.23), channel_id=1, source_target_pairs={{0,2},{1,3},{2,0},{3,1},{4,6},{5,7},{6,4},{7,5},{8,10},{9,11},{10,... | collective-permute-start | bytes 786440 | tf_op jit(solution)/shard_map/ppermute | solution.py:813
  24.1 9.2 %collective-permute-start.7 = (bf16[128,1024]{1,0:T(8,128)(2,1)S(1)}, bf16[128,1024]{1,0:T(8,128)(2,1)S(1)}, u32[]{:S(2)}, u32[]{:S(2)}) collective-permute-start(bf16[128,1024]{1,0:T(8,128)(2,1)S(1)} %copy-done.2), channel_id=1, source_target_pairs={{0,2},{1,3},{2,0},{3,1},{4,6},{5,7},{6,4},{7,5},{8,10},{9,11},{10,... | collective-permute-start | bytes 786440 | tf_op jit(solution)/shard_map/ppermute | solution.py:813
  36.6 9.0 %collective-permute-start.9 = (bf16[128,1024]{1,0:T(8,128)(2,1)}, bf16[128,1024]{1,0:T(8,128)(2,1)S(1)}, u32[]{:S(2)}, u32[]{:S(2)}) collective-permute-start(bf16[128,1024]{1,0:T(8,128)(2,1)} %get-tuple-element.99), channel_id=1, source_target_pairs={{0,1},{1,0},{2,3},{3,2},{4,5},{5,4},{6,7},{7,6},{8,9},{9,8},{10,11... | collective-permute-start | bytes 786440 | tf_op jit(solution)/shard_map/ppermute | solution.py:813
  45.6 11.7 %collective-permute-start.10 = (bf16[128,1024]{1,0:T(8,128)(2,1)S(1)}, bf16[128,1024]{1,0:T(8,128)(2,1)S(1)}, u32[]{:S(2)}, u32[]{:S(2)}) collective-permute-start(bf16[128,1024]{1,0:T(8,128)(2,1)S(1)} %add_convert_fusion.19), channel_id=1, source_target_pairs={{0,2},{1,3},{2,0},{3,1},{4,6},{5,7},{6,4},{7,5},{8,10},{9,11},{10,... | collective-permute-start | bytes 786440 | tf_op jit(solution)/shard_map/ppermute | solution.py:813
  48.0 11.8 %collective-permute-start.13 = (bf16[128,1024]{1,0:T(8,128)(2,1)S(1)}, bf16[128,1024]{1,0:T(8,128)(2,1)S(1)}, u32[]{:S(2)}, u32[]{:S(2)}) collective-permute-start(bf16[128,1024]{1,0:T(8,128)(2,1)S(1)} %add_convert_fusion.18.refs_10_), channel_id=1, source_target_pairs={{0,2},{1,3},{2,0},{3,1},{4,6},{5,7},{6,4},{7,5},{8,10},{9,11},{10,... | collective-permute-start | bytes 786440 | tf_op jit(solution)/shard_map/ppermute | solution.py:813
  57.4 5.1 %collective-permute-start.12 = (bf16[128,1024]{1,0:T(8,128)(2,1)S(1)}, bf16[128,1024]{1,0:T(8,128)(2,1)S(1)}, u32[]{:S(2)}, u32[]{:S(2)}) collective-permute-start(bf16[128,1024]{1,0:T(8,128)(2,1)S(1)} %add_convert_fusion.17.refs_11_.refs_12_), channel_id=1, source_target_pairs={{0,1},{1,0},{2,3},{3,2},{4,5},{5,4},{6,7},{7,6},{8,9},{9,8},{10,11... | collective-permute-start | bytes 786440 | tf_op jit(solution)/shard_map/ppermute | solution.py:813
  60.9 26.2 %collective-permute-start.16 = (bf16[32,128,128]{2,1,0:T(8,128)(2,1)}, bf16[32,128,128]{2,1,0:T(8,128)(2,1)}, u32[]{:S(2)}, u32[]{:S(2)}) collective-permute-start(bf16[32,128,128]{2,1,0:T(8,128)(2,1)} %get-tuple-element.120), channel_id=1, source_target_pairs={{0,4},{4,0},{8,12},{12,8},{16,20},{20,16},{24,28},{28,24},{1,5},{5... | collective-permute-start | bytes 3145736 | tf_op jit(solution)/shard_map/ppermute | solution.py:813
  83.2 11.8 %collective-permute-start.15 = (bf16[512,1024]{1,0:T(8,128)(2,1)}, bf16[512,1024]{1,0:T(8,128)(2,1)}, u32[]{:S(2)}, u32[]{:S(2)}) collective-permute-start(bf16[512,1024]{1,0:T(8,128)(2,1)} %get-tuple-element.119), channel_id=1, source_target_pairs={{0,1},{1,0},{2,3},{3,2},{4,5},{5,4},{6,7},{7,6},{8,9},{9,8},{10,11... | collective-permute-start | bytes 3145736 | tf_op jit(solution)/shard_map/ppermute | solution.py:813
  83.4 23.4 %collective-permute-start.18 = (bf16[28,128,128]{2,1,0:T(8,128)(2,1)}, bf16[28,128,128]{2,1,0:T(8,128)(2,1)S(1)}, u32[]{:S(2)}, u32[]{:S(2)}) collective-permute-start(bf16[28,128,128]{2,1,0:T(8,128)(2,1)} %get-tuple-element.125), channel_id=1, source_target_pairs={{0,4},{4,0},{8,12},{12,8},{16,20},{20,16},{24,28},{28,24},{1,5},{5... | collective-permute-start | bytes 2752520 | tf_op jit(solution)/shard_map/ppermute | solution.py:813
  84.7 15.1 %collective-permute-start.19 = (bf16[16,128,128]{2,1,0:T(8,128)(2,1)}, bf16[16,128,128]{2,1,0:T(8,128)(2,1)}, u32[]{:S(2)}, u32[]{:S(2)}) collective-permute-start(bf16[16,128,128]{2,1,0:T(8,128)(2,1)} %get-tuple-element.126), channel_id=1, source_target_pairs={{0,8},{4,12},{8,0},{12,4},{16,24},{20,28},{24,16},{28,20},{1,9},{5... | collective-permute-start | bytes 1572872 | tf_op jit(solution)/shard_map/ppermute | solution.py:813
  89.8 21.2 %collective-permute-start.22 = (bf16[16,128,128]{2,1,0:T(8,128)(2,1)}, bf16[16,128,128]{2,1,0:T(8,128)(2,1)}, u32[]{:S(2)}, u32[]{:S(2)}) collective-permute-start(bf16[16,128,128]{2,1,0:T(8,128)(2,1)} %get-tuple-element.189), channel_id=1, source_target_pairs={{0,8},{4,12},{8,0},{12,4},{16,24},{20,28},{24,16},{28,20},{1,9},{5... | collective-permute-start | bytes 1572872 | tf_op jit(solution)/shard_map/ppermute | solution.py:813
  93.2 27.6 %collective-permute-start.21 = (bf16[20,128,128]{2,1,0:T(8,128)(2,1)}, bf16[20,128,128]{2,1,0:T(8,128)(2,1)S(1)}, u32[]{:S(2)}, u32[]{:S(2)}) collective-permute-start(bf16[20,128,128]{2,1,0:T(8,128)(2,1)} %get-tuple-element.132), channel_id=1, source_target_pairs={{0,4},{4,0},{8,12},{12,8},{16,20},{20,16},{24,28},{28,24},{1,5},{5... | collective-permute-start | bytes 1966088 | tf_op jit(solution)/shard_map/ppermute | solution.py:813
  101.2 24.8 %collective-permute-start.26 = (bf16[8,128,128]{2,1,0:T(8,128)(2,1)S(1)}, bf16[8,128,128]{2,1,0:T(8,128)(2,1)S(1)}, u32[]{:S(2)}, u32[]{:S(2)}) collective-permute-start(bf16[8,128,128]{2,1,0:T(8,128)(2,1)S(1)} %get-tuple-element.197), channel_id=1, source_target_pairs={{0,4},{4,0},{8,12},{12,8},{16,20},{20,16},{24,28},{28,24},{1,5},{5... | collective-permute-start | bytes 786440 | tf_op jit(solution)/shard_map/ppermute | solution.py:813
  107.1 18.1 %collective-permute-start.20 = (bf16[14,128,128]{2,1,0:T(8,128)(2,1)S(1)}, bf16[14,128,128]{2,1,0:T(8,128)(2,1)S(1)}, u32[]{:S(2)}, u32[]{:S(2)}) collective-permute-start(bf16[14,128,128]{2,1,0:T(8,128)(2,1)S(1)} %get-tuple-element.190), channel_id=1, source_target_pairs={{0,8},{4,12},{8,0},{12,4},{16,24},{20,28},{24,16},{28,20},{1,9},{5... | collective-permute-start | bytes 1376264 | tf_op jit(solution)/shard_map/ppermute | solution.py:813
  112.7 25.6 %collective-permute-start.17 = (bf16[512,1024]{1,0:T(8,128)(2,1)S(1)}, bf16[512,1024]{1,0:T(8,128)(2,1)S(1)}, u32[]{:S(2)}, u32[]{:S(2)}) collective-permute-start(bf16[512,1024]{1,0:T(8,128)(2,1)S(1)} %add_convert_fusion.5), channel_id=1, source_target_pairs={{0,2},{1,3},{2,0},{3,1},{4,6},{5,7},{6,4},{7,5},{8,10},{9,11},{10,... | collective-permute-start | bytes 3145736 | tf_op jit(solution)/shard_map/ppermute | solution.py:813
  116.0 13.6 %collective-permute-start.25 = (bf16[8,128,128]{2,1,0:T(8,128)(2,1)S(1)}, bf16[8,128,128]{2,1,0:T(8,128)(2,1)S(1)}, u32[]{:S(2)}, u32[]{:S(2)}) collective-permute-start(bf16[8,128,128]{2,1,0:T(8,128)(2,1)S(1)} %get-tuple-element.195), channel_id=1, source_target_pairs={{0,16},{4,20},{8,24},{12,28},{16,0},{20,4},{24,8},{28,12},{1,17},{... | collective-permute-start | bytes 786440 | tf_op jit(solution)/shard_map/ppermute | solution.py:813
  121.0 16.5 %collective-permute-start.24 = (bf16[10,128,128]{2,1,0:T(8,128)(2,1)S(1)}, bf16[10,128,128]{2,1,0:T(8,128)(2,1)S(1)}, u32[]{:S(2)}, u32[]{:S(2)}) collective-permute-start(bf16[10,128,128]{2,1,0:T(8,128)(2,1)S(1)} %get-tuple-element.193), channel_id=1, source_target_pairs={{0,8},{4,12},{8,0},{12,4},{16,24},{20,28},{24,16},{28,20},{1,9},{5... | collective-permute-start | bytes 983048 | tf_op jit(solution)/shard_map/ppermute | solution.py:813
  126.0 12.2 %collective-permute-start.23 = (bf16[7,128,128]{2,1,0:T(8,128)(2,1)S(1)}, bf16[7,128,128]{2,1,0:T(8,128)(2,1)S(1)}, u32[]{:S(2)}, u32[]{:S(2)}) collective-permute-start(bf16[7,128,128]{2,1,0:T(8,128)(2,1)S(1)} %get-tuple-element.199), channel_id=1, source_target_pairs={{0,16},{4,20},{8,24},{12,28},{16,0},{20,4},{24,8},{28,12},{1,17},{... | collective-permute-start | bytes 688136 | tf_op jit(solution)/shard_map/ppermute | solution.py:813
  138.8 16.6 %collective-permute-start.29 = (bf16[4,128,128]{2,1,0:T(8,128)(2,1)S(1)}, bf16[4,128,128]{2,1,0:T(8,128)(2,1)S(1)}, u32[]{:S(2)}, u32[]{:S(2)}) collective-permute-start(bf16[4,128,128]{2,1,0:T(8,128)(2,1)S(1)} %get-tuple-element.203), channel_id=1, source_target_pairs={{0,16},{4,20},{8,24},{12,28},{16,0},{20,4},{24,8},{28,12},{1,17},{... | collective-permute-start | bytes 393224 | tf_op jit(solution)/shard_map/ppermute | solution.py:813
  140.7 14.7 %collective-permute-start.28 = (bf16[5,128,128]{2,1,0:T(8,128)(2,1)S(1)}, bf16[5,128,128]{2,1,0:T(8,128)(2,1)S(1)}, u32[]{:S(2)}, u32[]{:S(2)}) collective-permute-start(bf16[5,128,128]{2,1,0:T(8,128)(2,1)S(1)} %get-tuple-element.201), channel_id=1, source_target_pairs={{0,16},{4,20},{8,24},{12,28},{16,0},{20,4},{24,8},{28,12},{1,17},{... | collective-permute-start | bytes 491528 | tf_op jit(solution)/shard_map/ppermute | solution.py:813
  166.9 4.0 %collective-permute-start.32 = (f32[8,1024]{1,0:T(8,128)S(1)}, f32[8,1024]{1,0:T(8,128)S(1)}, u32[]{:S(2)}, u32[]{:S(2)}) collective-permute-start(f32[8,1024]{1,0:T(8,128)S(1)} %pad_add_fusion), channel_id=1, source_target_pairs={{0,4},{4,0},{8,12},{12,8},{16,20},{20,16},{24,28},{28,24},{1,5},{5... | collective-permute-start | bytes 98312 | tf_op jit(solution)/shard_map/ppermute | solution.py:813
  170.9 4.0 %collective-permute-start.33 = (f32[8,1024]{1,0:T(8,128)S(1)}, f32[8,1024]{1,0:T(8,128)S(1)}, u32[]{:S(2)}, u32[]{:S(2)}) collective-permute-start(f32[8,1024]{1,0:T(8,128)S(1)} %fusion.4), channel_id=1, source_target_pairs={{0,8},{4,12},{8,0},{12,4},{16,24},{20,28},{24,16},{28,20},{1,9},{5... | collective-permute-start | bytes 98312 | tf_op jit(solution)/shard_map/ppermute | solution.py:813
  174.9 5.2 %collective-permute-start.34 = (f32[8,1024]{1,0:T(8,128)S(1)}, f32[8,1024]{1,0:T(8,128)S(1)}, u32[]{:S(2)}, u32[]{:S(2)}) collective-permute-start(f32[8,1024]{1,0:T(8,128)S(1)} %add.162), channel_id=1, source_target_pairs={{0,16},{4,20},{8,24},{12,28},{16,0},{20,4},{24,8},{28,12},{1,17},{... | collective-permute-start | bytes 98312 | tf_op jit(solution)/shard_map/ppermute | solution.py:813
  (37 other events, 291.3 us)

commit v2 on v1

--- a/solution.py
+++ b/solution.py
@@ -295,7 +295,7 @@
     return ([entry], entry.shape[0], entry)
 
 
-def call(kernel, name, scalars, ins, outs, scratch=(), flops=0, after=None):
+def call(kernel, name, scalars, ins, outs, scratch=(), flops=0, after=None, limit=VMEM_LIMIT):
     operands = []
     shapes = []
     for entry in ins:
@@ -361,7 +361,7 @@
         + [pltpu.VMEM(shape, kind) for shape, kind, *_ in outs]
         + [pltpu.SemaphoreType.DMA((max(n_in, 1),)), pltpu.SemaphoreType.DMA((len(outs), SEMS))]
         + [pltpu.VMEM(shape, kind) for shape, kind in scratch],
-        compiler_params=pltpu.CompilerParams(vmem_limit_bytes=VMEM_LIMIT),
+        compiler_params=pltpu.CompilerParams(vmem_limit_bytes=limit),
         cost_estimate=pl.CostEstimate(flops=int(flops), bytes_accessed=0, transcendentals=0),
     )(*scalars, *operands)
 
@@ -727,28 +727,35 @@
     return (columns(left), right[:, None, :], coef_left, coef_right)
 
 
-def rotate_kernel(counts, group, me_ref, place_ref, loads, stores, found_ref):
-    left, right = loads[:2]
-    grads, turned, total = stores
-    parts = reflectors(left(), right())
+def collect_kernel(counts, group, me_ref, place_ref, loads, stores, found_ref):
+    grads, total = stores
     at = 0
     for number, count in enumerate(counts):
-        keep, got = loads[2 + 2 * number : 4 + 2 * number]
+        keep, got = loads[2 * number : 2 + 2 * number]
         found_ref[at : at + count] = keep()[...].astype(F32) + got()[...].astype(F32)
         at += count
     slots = grads.ref.shape[0]
-    for slot in range(slots):
-        grads.ref[slot] = found_ref[place_ref[me_ref[0] * slots + slot]]
-    grads.send()
     square = jnp.zeros((8, BLK), F32)
     for at in range(0, slots, group):
         rows = slice(at, at + group)
+        for slot in range(at, at + group):
+            grads.ref[slot] = found_ref[place_ref[me_ref[0] * slots + slot]]
+        grads.send(rows)
         grad = grads.ref[rows]
         square = square + jnp.sum((grad * grad).reshape(group * BLK // 8, 8, BLK), axis=0)
-        turned.ref[rows] = reflect(grad, *(part[rows] for part in parts))
-        turned.send(rows)
     total.ref[...] = jnp.full((8, BLK), jnp.sum(square), F32)
     total.send()
+
+
+def rotate_kernel(group, me_ref, loads, stores):
+    left, right, grads = loads
+    (turned,) = stores
+    parts = reflectors(left(), right())
+    grads_ref = grads()
+    for at in range(0, turned.ref.shape[0], group):
+        rows = slice(at, at + group)
+        turned.ref[rows] = reflect(grads_ref[rows], *(part[rows] for part in parts))
+        turned.send(rows)
 
 
 def inverse(value):
@@ -1184,14 +1191,24 @@
     right = right_vector.reshape(slots, BLK)
     block_f32 = ((slots, BLK, BLK), F32)
     group = 4 if slots % 4 == 0 else 1
-    grads, rotated, square = call(
-        functools.partial(rotate_kernel, counts, group),
-        "rotate",
+    grads, square = call(
+        functools.partial(collect_kernel, counts, group),
+        "collect",
         (me, place),
-        (left, right, *pending),
-        [block_f32, block_f32, ((8, BLK), F32)],
+        tuple(pending),
+        [block_f32, ((8, BLK), F32)],
         [((sum(counts), BLK, BLK), F32)],
         flops=unit,
+        limit=40 * MIB,
+    )
+    (rotated,) = call(
+        functools.partial(rotate_kernel, group),
+        "rotate",
+        (me,),
+        (left, right, grads),
+        [block_f32],
+        flops=unit,
+        limit=40 * MIB,
     )
     bit = 1
     while bit < lax.axis_size("mp"):
@@ -1228,6 +1245,7 @@
             ((1, 1), F32),
         ],
         flops=unit,
+        limit=40 * MIB,
     )
     shard_shape = (slots, 1, BLK, BLK)
     return (

time: 191 us -> 186 us (0.974)
  other arithmetic: 20.2 us -> 15.6 us
    convert_element_type x18, other arithmetic: 15.9 us -> 13.1 us  [plus(): return (left.astype(F32) + right.astype(F32)).astype(BF16)]
    unnamed x58 -> x68, local copies, waits for them, and re-layouts: 3.95 us -> 2.31 us
    pallas_call x9 -> x10, Pallas kernels: 81.9 us -> 82.4 us  [call(): pl.pallas_call(body, name=name, out_shape=results, in_specs=[pl.BlockSpec...]
  transfers between devices with their start and end apart: 32 -> 32, of which waited for: 15 -> 14; matrix products, arithmetic and copies ran while one was open for 11% -> 9% of each run, Pallas kernels for 30% -> 32%
where the time goes in v2:
time: 186 us
  Pallas kernels  82.4 us (44%)
  waiting for transfers between devices  46.4 us (25%)
  starting transfers between devices  32.3 us (17%)
  other arithmetic  15.6 us (8%)
  local copies, waits for them, and re-layouts  4.8 us (3%)
  between operations  4.13 us (2%)
    pallas_call x10, Pallas kernels, call(): pl.pallas_call(body, name=name, out_shape=results, in_specs=[pl.BlockSpec...  82.4 us
    ppermute x32, waiting for transfers between devices, swap(): return lax.ppermute(value, axis, [(i, i ^ bit) for i in range(count)])  46.4 us
    ppermute x32, starting transfers between devices, swap(): return lax.ppermute(value, axis, [(i, i ^ bit) for i in range(count)])  32.3 us
    convert_element_type x18, other arithmetic, plus(): return (left.astype(F32) + right.astype(F32)).astype(BF16)  13.1 us
  transfers between devices with their start and end apart: 32, of which 14 were waited for; matrix products, arithmetic and copies ran while one was open for 9% of the time, Pallas kernels for 32%

profile of v2, /device:TPU:0, one launch (start us, length us, event | category | flops | bytes accessed | tf_op | source)
XLA Modules:
  0.0 185.7 jit_solution(5998915000685011961)
XLA Ops:
  0.7 10.3 %attention_forward.1 = (bf16[512,1024]{1,0:T(8,128)(2,1)}, bf16[512,256]{1,0:T(8,128)(2,1)}, bf16[512,256]{1,0:T(8,128)(2,1)}, bf16[512,256]{1,0:T(8,128)(2,1)},...) custom-call(s32[2]{0:T(128)S(1)} %pad_add_fusion.3.refs_0_, ...), custom_call_target="tpu_custom_call" | custom-call | flops 5368709120 | tf_op jit(solution)/shard_map/attention_forward/pallas_call | solution.py:354
  13.9 2.9 %collective-permute-start.4 = (bf16[128,1024]{1,0:T(8,128)(2,1)S(1)}, bf16[128,1024]{1,0:T(8,128)(2,1)S(1)}, u32[]{:S(2)}, u32[]{:S(2)}) collective-permute-start(bf16[128,1024]{1,0:T(8,128)(2,1)S(1)} %add_convert_fusion.23), channel_id=1, source_target_pairs={{0,2},{1,3},{2,0},{3,1},{4,6},{5,7},{6,4},{7,5},{8,10},{9,11},{10,... | collective-permute-start | bytes 786440 | tf_op jit(solution)/shard_map/ppermute | solution.py:820
  18.6 5.2 %grad_of_act.1 = (bf16[512,1024]{1,0:T(8,128)(2,1)}, f32[512,1024]{1,0:T(8,128)}) custom-call(s32[2]{0:T(128)S(1)} %pad_add_fusion.3.refs_0_, s32[1,512]{1,0:T(1,128)} %bitcast.41, bf16[512,1024]{1,0:T(8,128)(2,1)} %refs_2_.4, bf16[1024,1024]{1,0:T(8,128)(2,1)} %refs_30_.1, bf16[128,1024]{1,0:T(8,128)(2,1)} %add_convert_fusion.22.refs_4_), custom_call_target="tpu_custom_call" | custom-call | flops 2147483648 | tf_op jit(solution)/shard_map/grad_of_act/pallas_call | solution.py:354
  26.2 7.1 %feed_forward_a.1 = (bf16[256,1024]{1,0:T(8,128)(2,1)}, bf16[256,1024]{1,0:T(8,128)(2,1)}, bf16[256,1024]{1,0:T(8,128)(2,1)}, bf16[128,1024]{1,0:T(8,128)(2,1)}, bf16[128,1024]{1,0:T(8,128)(2,1)}) custom-call(s32[2]{0:T(128)S(1)} %pad_add_fusion.3.refs_0_, s32[1,512]{1,0:T(1,128)} %bitcast.44, bf16[192,512]{1,0:T(8,128)(2,1)} %constant.42.clone.refs_2_.refs_4_.refs_3_, ...), custom_call_target="tpu_custom_call" | custom-call | flops 4294967296 | tf_op jit(solution)/shard_map/feed_forward_a/pallas_call | solution.py:354
  37.6 7.0 %feed_forward_b.1 = (bf16[256,1024]{1,0:T(8,128)(2,1)}, bf16[256,1024]{1,0:T(8,128)(2,1)}, bf16[256,1024]{1,0:T(8,128)(2,1)}, bf16[128,1024]{1,0:T(8,128)(2,1)}, bf16[128,1024]{1,0:T(8,128)(2,1)}) custom-call(s32[2]{0:T(128)S(1)} %pad_add_fusion.3.refs_0_, s32[1,512]{1,0:T(1,128)} %bitcast.45, bf16[192,512]{1,0:T(8,128)(2,1)} %constant.42.clone.refs_2_.refs_4_.refs_3_, ...), custom_call_target="tpu_custom_call" | custom-call | flops 4294967296 | tf_op jit(solution)/shard_map/feed_forward_b/pallas_call | solution.py:354
  48.9 8.4 %feed_weight_grads.1 = (bf16[80,128,128]{2,1,0:T(8,128)(2,1)}, bf16[32,128,128]{2,1,0:T(8,128)(2,1)}, bf16[32,128,128]{2,1,0:T(8,128)(2,1)}) custom-call(s32[2]{0:T(128)S(1)} %pad_add_fusion.3.refs_0_, s32[336]{0:T(512)S(1)} %pad_add_fusion.2.refs_1_, f32[4]{0:T(128)} %pad_maximum_fusion.refs_2_.refs_1_, bf16[256,1024]{1,0:T(8,128)(2,1)} %get-tuple-element.99.refs_3_, ...), custom_call_target="tpu_custom_call" | custom-call | flops 4294967296 | tf_op jit(solution)/shard_map/feed_weight_grads/pallas_call | solution.py:354
  57.5 2.3 %collective-permute-done.13 = bf16[128,1024]{1,0:T(8,128)(2,1)S(1)} collective-permute-done((bf16[128,1024]{1,0:T(8,128)(2,1)S(1)}, bf16[128,1024]{1,0:T(8,128)(2,1)S(1)}, u32[]{:S(2)}, u32[]{:S(2)}) %collective-permute-start.13) | collective-permute-done | bytes 262176 | tf_op jit(solution)/shard_map/ppermute | solution.py:820
  63.3 19.8 %attention_backward.1 = (bf16[64,128,128]{2,1,0:T(8,128)(2,1)S(1)}, bf16[512,1024]{1,0:T(8,128)(2,1)}, bf16[512,1024]{1,0:T(8,128)(2,1)}, bf16[28,128,128]{2,1,0...) custom-call(s32[2]{0:T(128)S(1)} %pad_add_fusion.3.refs_0_, ...), custom_call_target="tpu_custom_call" | custom-call | flops 10737418240 | tf_op jit(solution)/shard_map/attention_backward/pallas_call | solution.py:354
  87.6 2.7 %add_convert_fusion.6 = (bf16[16,128,128]{2,1,0:T(8,128)(2,1)S(1)}, bf16[16,128,128]{2,1,0:T(8,128)(2,1)}) fusion(bf16[32,128,128]{2,1,0:T(8,128)(2,1)} %collective-permute-done.16, bf16[32,128,128]{2,1,0:T(8,128)(2,1)} %get-tuple-element.121), kind=kLoop, calls=%fused_computation.6 | loop fusion | flops 2097152 | bytes 3145728 | tf_op jit(solution)/shard_map/convert_element_type | solution.py:824
  94.4 5.4 %collective-permute-done.19 = bf16[16,128,128]{2,1,0:T(8,128)(2,1)} collective-permute-done((bf16[16,128,128]{2,1,0:T(8,128)(2,1)}, bf16[16,128,128]{2,1,0:T(8,128)(2,1)}, u32[]{:S(2)}, u32[]{:S(2)}) %collective-permute-start.19) | collective-permute-done | bytes 524320 | tf_op jit(solution)/shard_map/ppermute | solution.py:820
  102.0 4.8 %collective-permute-done.18 = bf16[28,128,128]{2,1,0:T(8,128)(2,1)S(1)} collective-permute-done((bf16[28,128,128]{2,1,0:T(8,128)(2,1)}, bf16[28,128,128]{2,1,0:T(8,128)(2,1)S(1)}, u32[]{:S(2)}, u32[]{:S(2)}) %collective-permute-start.18) | collective-permute-done | bytes 917536 | tf_op jit(solution)/shard_map/ppermute | solution.py:820
  115.2 2.7 %collective-permute-start.25 = (bf16[8,128,128]{2,1,0:T(8,128)(2,1)S(1)}, bf16[8,128,128]{2,1,0:T(8,128)(2,1)S(1)}, u32[]{:S(2)}, u32[]{:S(2)}) collective-permute-start(bf16[8,128,128]{2,1,0:T(8,128)(2,1)S(1)} %get-tuple-element.193), channel_id=1, source_target_pairs={{0,16},{4,20},{8,24},{12,28},{16,0},{20,4},{24,8},{28,12},{1,17},{... | collective-permute-start | bytes 786440 | tf_op jit(solution)/shard_map/ppermute | solution.py:820
  118.0 2.9 %collective-permute-done.21 = bf16[20,128,128]{2,1,0:T(8,128)(2,1)S(1)} collective-permute-done((bf16[20,128,128]{2,1,0:T(8,128)(2,1)}, bf16[20,128,128]{2,1,0:T(8,128)(2,1)S(1)}, u32[]{:S(2)}, u32[]{:S(2)}) %collective-permute-start.21) | collective-permute-done | bytes 655392 | tf_op jit(solution)/shard_map/ppermute | solution.py:820
  122.7 3.1 %collective-permute-done.20 = bf16[14,128,128]{2,1,0:T(8,128)(2,1)S(1)} collective-permute-done((bf16[14,128,128]{2,1,0:T(8,128)(2,1)S(1)}, bf16[14,128,128]{2,1,0:T(8,128)(2,1)S(1)}, u32[]{:S(2)}, u32[]{:S(2)}) %collective-permute-start.20) | collective-permute-done | bytes 458784 | tf_op jit(solution)/shard_map/ppermute | solution.py:820
  127.9 9.5 %collective-permute-done.24 = bf16[10,128,128]{2,1,0:T(8,128)(2,1)S(1)} collective-permute-done((bf16[10,128,128]{2,1,0:T(8,128)(2,1)S(1)}, bf16[10,128,128]{2,1,0:T(8,128)(2,1)S(1)}, u32[]{:S(2)}, u32[]{:S(2)}) %collective-permute-start.24) | collective-permute-done | bytes 327712 | tf_op jit(solution)/shard_map/ppermute | solution.py:820
  138.1 2.6 %collective-permute-start.29 = (bf16[4,128,128]{2,1,0:T(8,128)(2,1)S(1)}, bf16[4,128,128]{2,1,0:T(8,128)(2,1)S(1)}, u32[]{:S(2)}, u32[]{:S(2)}) collective-permute-start(bf16[4,128,128]{2,1,0:T(8,128)(2,1)S(1)} %get-tuple-element.201), channel_id=1, source_target_pairs={{0,16},{4,20},{8,24},{12,28},{16,0},{20,4},{24,8},{28,12},{1,17},{... | collective-permute-start | bytes 393224 | tf_op jit(solution)/shard_map/ppermute | solution.py:820
  141.1 9.2 %layer_outputs.1 = (f32[512,1024]{1,0:T(8,128)}, f32[512,1024]{1,0:T(8,128)}, f32[8,1024]{1,0:T(8,128)}) custom-call(s32[2]{0:T(128)S(1)} %copy-done.28, f32[4]{0:T(128)} %pad_maximum_fusion.refs_2_.refs_1_, s32[1,512]{1,0:T(1,128)} %bitcast.47, bf16[192,512]{1,0:T(8,128)(2,1)} %constant.42.clone.refs_2_.refs_4_.refs_3_, bf16[512,1024]{1,0:T(8,128)(2,1)} %refs_4_.3, ...), custom_call_target="tpu_custom_call" | custom-call | flops 2147483648 | tf_op jit(solution)/shard_map/layer_outputs/pallas_call | solution.py:354
  150.3 4.4 %collective-permute-done.28.refs_7_ = bf16[5,128,128]{2,1,0:T(8,128)(2,1)S(1)} collective-permute-done((bf16[5,128,128]{2,1,0:T(8,128)(2,1)S(1)}, bf16[5,128,128]{2,1,0:T(8,128)(2,1)S(1)}, u32[]{:S(2)}, u32[]{:S(2)}) %collective-permute-start.28) | collective-permute-done | bytes 163872 | tf_op jit(solution)/shard_map/ppermute | solution.py:820
  154.8 4.2 %collect.1 = (f32[24,128,128]{2,1,0:T(8,128)S(1)}, f32[8,128]{1,0:T(8,128)S(1)}) custom-call(s32[2]{0:T(128)S(1)} %copy-done.28, s32[192]{0:T(256)S(1)} %compare_select_fusion.1.refs_1_, bf16[8,128,128]{2,1,0:T(8,128)(2,1)S(1)} %get-tuple-element.192.refs_2_, bf16[8,128,128]{2,1,0:T(8,128)(2,1)S(1)} %collective-permute-done.25.refs_3_, ...), custom_call_target="tpu_custom_call" | custom-call | flops 1073741824 | tf_op jit(solution)/shard_map/collect/pallas_call | solution.py:354
  164.8 3.0 %collective-permute-done.32 = f32[8,1024]{1,0:T(8,128)S(1)} collective-permute-done((f32[8,1024]{1,0:T(8,128)S(1)}, f32[8,1024]{1,0:T(8,128)S(1)}, u32[]{:S(2)}, u32[]{:S(2)}) %collective-permute-start.32) | collective-permute-done | bytes 32800 | tf_op jit(solution)/shard_map/ppermute | solution.py:820
  168.5 3.3 %collective-permute-done.33 = f32[8,1024]{1,0:T(8,128)S(1)} collective-permute-done((f32[8,1024]{1,0:T(8,128)S(1)}, f32[8,1024]{1,0:T(8,128)S(1)}, u32[]{:S(2)}, u32[]{:S(2)}) %collective-permute-start.33) | collective-permute-done | bytes 32800 | tf_op jit(solution)/shard_map/ppermute | solution.py:820
  171.9 2.2 %collective-permute-start.34 = (f32[8,1024]{1,0:T(8,128)S(1)}, f32[8,1024]{1,0:T(8,128)S(1)}, u32[]{:S(2)}, u32[]{:S(2)}) collective-permute-start(f32[8,1024]{1,0:T(8,128)S(1)} %add.162), channel_id=1, source_target_pairs={{0,16},{4,20},{8,24},{12,28},{16,0},{20,4},{24,8},{28,12},{1,17},{... | collective-permute-start | bytes 98312 | tf_op jit(solution)/shard_map/ppermute | solution.py:820
  174.1 3.1 %rotate.1.refs_9_ = f32[24,128,128]{2,1,0:T(8,128)S(1)} custom-call(s32[2]{0:T(128)S(1)} %copy-done.28, f32[24,128]{1,0:T(8,128)S(1)} %bitcast.30, f32[24,128]{1,0:T(8,128)S(1)} %bitcast.32, f32[24,128,128]{2,1,0:T(8,128)S(1)} %get-tuple-element.148.refs_3_.refs_8_), custom_call_target="tpu_custom_call" | custom-call | flops 1073741824 | tf_op jit(solution)/shard_map/rotate/pallas_call | solution.py:354
  177.3 8.2 %update.1 = (f32[24,128,128]{2,1,0:T(8,128)}, f32[24,128,128]{2,1,0:T(8,128)}, f32[24,128,128]{2,1,0:T(8,128)}, f32[24,128,128]{2,1,0:T(8,128)}, bf16[24,128,128...) custom-call(s32[2]{0:T(128)S(1)} %copy-done.28, ...), custom_call_target="tpu_custom_call" | custom-call | flops 1073741824 | tf_op jit(solution)/shard_map/update/pallas_call | solution.py:354
  (171 shorter events, 47.9 us)
Async XLA Ops:
  11.5 5.3 %collective-permute-start.5 = (bf16[128,1024]{1,0:T(8,128)(2,1)}, bf16[128,1024]{1,0:T(8,128)(2,1)S(1)}, u32[]{:S(2)}, u32[]{:S(2)}) collective-permute-start(bf16[128,1024]{1,0:T(8,128)(2,1)} %get-tuple-element.93), channel_id=1, source_target_pairs={{0,1},{1,0},{2,3},{3,2},{4,5},{5,4},{6,7},{7,6},{8,9},{9,8},{10,11... | collective-permute-start | bytes 786440 | tf_op jit(solution)/shard_map/ppermute | solution.py:820
  13.9 9.8 %collective-permute-start.4 = (bf16[128,1024]{1,0:T(8,128)(2,1)S(1)}, bf16[128,1024]{1,0:T(8,128)(2,1)S(1)}, u32[]{:S(2)}, u32[]{:S(2)}) collective-permute-start(bf16[128,1024]{1,0:T(8,128)(2,1)S(1)} %add_convert_fusion.23), channel_id=1, source_target_pairs={{0,2},{1,3},{2,0},{3,1},{4,6},{5,7},{6,4},{7,5},{8,10},{9,11},{10,... | collective-permute-start | bytes 786440 | tf_op jit(solution)/shard_map/ppermute | solution.py:820
  24.1 9.2 %collective-permute-start.7 = (bf16[128,1024]{1,0:T(8,128)(2,1)S(1)}, bf16[128,1024]{1,0:T(8,128)(2,1)S(1)}, u32[]{:S(2)}, u32[]{:S(2)}) collective-permute-start(bf16[128,1024]{1,0:T(8,128)(2,1)S(1)} %copy-done.11), channel_id=1, source_target_pairs={{0,2},{1,3},{2,0},{3,1},{4,6},{5,7},{6,4},{7,5},{8,10},{9,11},{10,... | collective-permute-start | bytes 786440 | tf_op jit(solution)/shard_map/ppermute | solution.py:820
  36.5 9.0 %collective-permute-start.9 = (bf16[128,1024]{1,0:T(8,128)(2,1)}, bf16[128,1024]{1,0:T(8,128)(2,1)S(1)}, u32[]{:S(2)}, u32[]{:S(2)}) collective-permute-start(bf16[128,1024]{1,0:T(8,128)(2,1)} %get-tuple-element.98), channel_id=1, source_target_pairs={{0,1},{1,0},{2,3},{3,2},{4,5},{5,4},{6,7},{7,6},{8,9},{9,8},{10,11... | collective-permute-start | bytes 786440 | tf_op jit(solution)/shard_map/ppermute | solution.py:820
  45.6 11.7 %collective-permute-start.10 = (bf16[128,1024]{1,0:T(8,128)(2,1)S(1)}, bf16[128,1024]{1,0:T(8,128)(2,1)S(1)}, u32[]{:S(2)}, u32[]{:S(2)}) collective-permute-start(bf16[128,1024]{1,0:T(8,128)(2,1)S(1)} %add_convert_fusion.19), channel_id=1, source_target_pairs={{0,2},{1,3},{2,0},{3,1},{4,6},{5,7},{6,4},{7,5},{8,10},{9,11},{10,... | collective-permute-start | bytes 786440 | tf_op jit(solution)/shard_map/ppermute | solution.py:820
  48.0 11.8 %collective-permute-start.13 = (bf16[128,1024]{1,0:T(8,128)(2,1)S(1)}, bf16[128,1024]{1,0:T(8,128)(2,1)S(1)}, u32[]{:S(2)}, u32[]{:S(2)}) collective-permute-start(bf16[128,1024]{1,0:T(8,128)(2,1)S(1)} %add_convert_fusion.18.refs_10_), channel_id=1, source_target_pairs={{0,2},{1,3},{2,0},{3,1},{4,6},{5,7},{6,4},{7,5},{8,10},{9,11},{10,... | collective-permute-start | bytes 786440 | tf_op jit(solution)/shard_map/ppermute | solution.py:820
  57.4 5.1 %collective-permute-start.12 = (bf16[128,1024]{1,0:T(8,128)(2,1)S(1)}, bf16[128,1024]{1,0:T(8,128)(2,1)S(1)}, u32[]{:S(2)}, u32[]{:S(2)}) collective-permute-start(bf16[128,1024]{1,0:T(8,128)(2,1)S(1)} %add_convert_fusion.17.refs_11_.refs_12_), channel_id=1, source_target_pairs={{0,1},{1,0},{2,3},{3,2},{4,5},{5,4},{6,7},{7,6},{8,9},{9,8},{10,11... | collective-permute-start | bytes 786440 | tf_op jit(solution)/shard_map/ppermute | solution.py:820
  60.9 26.7 %collective-permute-start.16 = (bf16[32,128,128]{2,1,0:T(8,128)(2,1)}, bf16[32,128,128]{2,1,0:T(8,128)(2,1)}, u32[]{:S(2)}, u32[]{:S(2)}) collective-permute-start(bf16[32,128,128]{2,1,0:T(8,128)(2,1)} %get-tuple-element.119), channel_id=1, source_target_pairs={{0,4},{4,0},{8,12},{12,8},{16,20},{20,16},{24,28},{28,24},{1,5},{5... | collective-permute-start | bytes 3145736 | tf_op jit(solution)/shard_map/ppermute | solution.py:820
  83.2 11.3 %collective-permute-start.15 = (bf16[512,1024]{1,0:T(8,128)(2,1)}, bf16[512,1024]{1,0:T(8,128)(2,1)}, u32[]{:S(2)}, u32[]{:S(2)}) collective-permute-start(bf16[512,1024]{1,0:T(8,128)(2,1)} %get-tuple-element.118), channel_id=1, source_target_pairs={{0,1},{1,0},{2,3},{3,2},{4,5},{5,4},{6,7},{7,6},{8,9},{9,8},{10,11... | collective-permute-start | bytes 3145736 | tf_op jit(solution)/shard_map/ppermute | solution.py:820
  83.4 23.4 %collective-permute-start.18 = (bf16[28,128,128]{2,1,0:T(8,128)(2,1)}, bf16[28,128,128]{2,1,0:T(8,128)(2,1)S(1)}, u32[]{:S(2)}, u32[]{:S(2)}) collective-permute-start(bf16[28,128,128]{2,1,0:T(8,128)(2,1)} %get-tuple-element.124), channel_id=1, source_target_pairs={{0,4},{4,0},{8,12},{12,8},{16,20},{20,16},{24,28},{28,24},{1,5},{5... | collective-permute-start | bytes 2752520 | tf_op jit(solution)/shard_map/ppermute | solution.py:820
  84.7 15.1 %collective-permute-start.19 = (bf16[16,128,128]{2,1,0:T(8,128)(2,1)}, bf16[16,128,128]{2,1,0:T(8,128)(2,1)}, u32[]{:S(2)}, u32[]{:S(2)}) collective-permute-start(bf16[16,128,128]{2,1,0:T(8,128)(2,1)} %get-tuple-element.125), channel_id=1, source_target_pairs={{0,8},{4,12},{8,0},{12,4},{16,24},{20,28},{24,16},{28,20},{1,9},{5... | collective-permute-start | bytes 1572872 | tf_op jit(solution)/shard_map/ppermute | solution.py:820
  90.3 20.7 %collective-permute-start.22 = (bf16[16,128,128]{2,1,0:T(8,128)(2,1)}, bf16[16,128,128]{2,1,0:T(8,128)(2,1)}, u32[]{:S(2)}, u32[]{:S(2)}) collective-permute-start(bf16[16,128,128]{2,1,0:T(8,128)(2,1)} %get-tuple-element.187), channel_id=1, source_target_pairs={{0,8},{4,12},{8,0},{12,4},{16,24},{20,28},{24,16},{28,20},{1,9},{5... | collective-permute-start | bytes 1572872 | tf_op jit(solution)/shard_map/ppermute | solution.py:820
  92.7 28.1 %collective-permute-start.21 = (bf16[20,128,128]{2,1,0:T(8,128)(2,1)}, bf16[20,128,128]{2,1,0:T(8,128)(2,1)S(1)}, u32[]{:S(2)}, u32[]{:S(2)}) collective-permute-start(bf16[20,128,128]{2,1,0:T(8,128)(2,1)} %get-tuple-element.131), channel_id=1, source_target_pairs={{0,4},{4,0},{8,12},{12,8},{16,20},{20,16},{24,28},{28,24},{1,5},{5... | collective-permute-start | bytes 1966088 | tf_op jit(solution)/shard_map/ppermute | solution.py:820
  101.3 24.8 %collective-permute-start.26 = (bf16[8,128,128]{2,1,0:T(8,128)(2,1)S(1)}, bf16[8,128,128]{2,1,0:T(8,128)(2,1)S(1)}, u32[]{:S(2)}, u32[]{:S(2)}) collective-permute-start(bf16[8,128,128]{2,1,0:T(8,128)(2,1)S(1)} %get-tuple-element.195), channel_id=1, source_target_pairs={{0,4},{4,0},{8,12},{12,8},{16,20},{20,16},{24,28},{28,24},{1,5},{5... | collective-permute-start | bytes 786440 | tf_op jit(solution)/shard_map/ppermute | solution.py:820
  107.1 18.7 %collective-permute-start.20 = (bf16[14,128,128]{2,1,0:T(8,128)(2,1)S(1)}, bf16[14,128,128]{2,1,0:T(8,128)(2,1)S(1)}, u32[]{:S(2)}, u32[]{:S(2)}) collective-permute-start(bf16[14,128,128]{2,1,0:T(8,128)(2,1)S(1)} %get-tuple-element.188), channel_id=1, source_target_pairs={{0,8},{4,12},{8,0},{12,4},{16,24},{20,28},{24,16},{28,20},{1,9},{5... | collective-permute-start | bytes 1376264 | tf_op jit(solution)/shard_map/ppermute | solution.py:820
  112.6 25.0 %collective-permute-start.17 = (bf16[512,1024]{1,0:T(8,128)(2,1)S(1)}, bf16[512,1024]{1,0:T(8,128)(2,1)S(1)}, u32[]{:S(2)}, u32[]{:S(2)}) collective-permute-start(bf16[512,1024]{1,0:T(8,128)(2,1)S(1)} %add_convert_fusion.5), channel_id=1, source_target_pairs={{0,2},{1,3},{2,0},{3,1},{4,6},{5,7},{6,4},{7,5},{8,10},{9,11},{10,... | collective-permute-start | bytes 3145736 | tf_op jit(solution)/shard_map/ppermute | solution.py:820
  115.2 12.7 %collective-permute-start.25 = (bf16[8,128,128]{2,1,0:T(8,128)(2,1)S(1)}, bf16[8,128,128]{2,1,0:T(8,128)(2,1)S(1)}, u32[]{:S(2)}, u32[]{:S(2)}) collective-permute-start(bf16[8,128,128]{2,1,0:T(8,128)(2,1)S(1)} %get-tuple-element.193), channel_id=1, source_target_pairs={{0,16},{4,20},{8,24},{12,28},{16,0},{20,4},{24,8},{28,12},{1,17},{... | collective-permute-start | bytes 786440 | tf_op jit(solution)/shard_map/ppermute | solution.py:820
  121.0 16.5 %collective-permute-start.24 = (bf16[10,128,128]{2,1,0:T(8,128)(2,1)S(1)}, bf16[10,128,128]{2,1,0:T(8,128)(2,1)S(1)}, u32[]{:S(2)}, u32[]{:S(2)}) collective-permute-start(bf16[10,128,128]{2,1,0:T(8,128)(2,1)S(1)} %get-tuple-element.191), channel_id=1, source_target_pairs={{0,8},{4,12},{8,0},{12,4},{16,24},{20,28},{24,16},{28,20},{1,9},{5... | collective-permute-start | bytes 983048 | tf_op jit(solution)/shard_map/ppermute | solution.py:820
  125.9 11.6 %collective-permute-start.23 = (bf16[7,128,128]{2,1,0:T(8,128)(2,1)S(1)}, bf16[7,128,128]{2,1,0:T(8,128)(2,1)S(1)}, u32[]{:S(2)}, u32[]{:S(2)}) collective-permute-start(bf16[7,128,128]{2,1,0:T(8,128)(2,1)S(1)} %get-tuple-element.197), channel_id=1, source_target_pairs={{0,16},{4,20},{8,24},{12,28},{16,0},{20,4},{24,8},{28,12},{1,17},{... | collective-permute-start | bytes 688136 | tf_op jit(solution)/shard_map/ppermute | solution.py:820
  138.1 16.6 %collective-permute-start.29 = (bf16[4,128,128]{2,1,0:T(8,128)(2,1)S(1)}, bf16[4,128,128]{2,1,0:T(8,128)(2,1)S(1)}, u32[]{:S(2)}, u32[]{:S(2)}) collective-permute-start(bf16[4,128,128]{2,1,0:T(8,128)(2,1)S(1)} %get-tuple-element.201), channel_id=1, source_target_pairs={{0,16},{4,20},{8,24},{12,28},{16,0},{20,4},{24,8},{28,12},{1,17},{... | collective-permute-start | bytes 393224 | tf_op jit(solution)/shard_map/ppermute | solution.py:820
  140.7 14.1 %collective-permute-start.28 = (bf16[5,128,128]{2,1,0:T(8,128)(2,1)S(1)}, bf16[5,128,128]{2,1,0:T(8,128)(2,1)S(1)}, u32[]{:S(2)}, u32[]{:S(2)}) collective-permute-start(bf16[5,128,128]{2,1,0:T(8,128)(2,1)S(1)} %get-tuple-element.199), channel_id=1, source_target_pairs={{0,16},{4,20},{8,24},{12,28},{16,0},{20,4},{24,8},{28,12},{1,17},{... | collective-permute-start | bytes 491528 | tf_op jit(solution)/shard_map/ppermute | solution.py:820
  163.8 4.0 %collective-permute-start.32 = (f32[8,1024]{1,0:T(8,128)S(1)}, f32[8,1024]{1,0:T(8,128)S(1)}, u32[]{:S(2)}, u32[]{:S(2)}) collective-permute-start(f32[8,1024]{1,0:T(8,128)S(1)} %pad_add_fusion), channel_id=1, source_target_pairs={{0,4},{4,0},{8,12},{12,8},{16,20},{20,16},{24,28},{28,24},{1,5},{5... | collective-permute-start | bytes 98312 | tf_op jit(solution)/shard_map/ppermute | solution.py:820
  167.9 4.0 %collective-permute-start.33 = (f32[8,1024]{1,0:T(8,128)S(1)}, f32[8,1024]{1,0:T(8,128)S(1)}, u32[]{:S(2)}, u32[]{:S(2)}) collective-permute-start(f32[8,1024]{1,0:T(8,128)S(1)} %fusion.4), channel_id=1, source_target_pairs={{0,8},{4,12},{8,0},{12,4},{16,24},{20,28},{24,16},{28,20},{1,9},{5... | collective-permute-start | bytes 98312 | tf_op jit(solution)/shard_map/ppermute | solution.py:820
  171.9 5.3 %collective-permute-start.34 = (f32[8,1024]{1,0:T(8,128)S(1)}, f32[8,1024]{1,0:T(8,128)S(1)}, u32[]{:S(2)}, u32[]{:S(2)}) collective-permute-start(f32[8,1024]{1,0:T(8,128)S(1)} %add.162), channel_id=1, source_target_pairs={{0,16},{4,20},{8,24},{12,28},{16,0},{20,4},{24,8},{28,12},{1,17},{... | collective-permute-start | bytes 98312 | tf_op jit(solution)/shard_map/ppermute | solution.py:820
  (42 other events, 371.3 us)

commit v3 on v2

--- a/solution.py
+++ b/solution.py
@@ -1011,6 +1011,7 @@
             [((half, units), F32)],
             flops=4 * unit,
             after=token,
+            limit=50 * MIB,
         )
 
     second_a, act_a, gpre_a, keep_a, send_a = feed(0, "feed_forward_a", attn_a, None)
@@ -1029,6 +1030,7 @@
         [((count, BLK, BLK), BF16)] + chunk_e,
         [((blocks - late_count, BLK, BLK), BF16)],
         flops=4 * unit,
+        limit=48 * MIB,
         after=near_b,
     )
     far_a = mp_far(near_a, rest)
@@ -1133,6 +1135,7 @@
             [(rows_d, F32), (rows_d, F32), ((8, D), F32)],
             [(half_d, F32), ((32, D), F32)],
             flops=2 * unit,
+            limit=40 * MIB,
         )
         last.append(outputs[2])
         return outputs
@@ -1167,7 +1170,7 @@
 
     plan = ["near", "far", "finish"]
     if early_slots and stages == 3:
-        plan = ["near",(3,0),(1,0),(0,1),(2,0),(1,1),(3,1),(0,2),(2,1),(1,2),"far","finish"]
+        plan = ["near",(3,0),(1,0),(0,1),(2,0),(1,1),(0,2),(3,1),(2,1),(1,2),"far","finish"]
     plan += [(i, d - i) for d in range(len(state) + stages) for i in range(len(state))]
     for entry in plan:
         if entry == "near":
@@ -1199,7 +1202,7 @@
         [block_f32, ((8, BLK), F32)],
         [((sum(counts), BLK, BLK), F32)],
         flops=unit,
-        limit=40 * MIB,
+        limit=28 * MIB,
     )
     (rotated,) = call(
         functools.partial(rotate_kernel, group),
@@ -1208,7 +1211,7 @@
         (left, right, grads),
         [block_f32],
         flops=unit,
-        limit=40 * MIB,
+        limit=28 * MIB,
     )
     bit = 1
     while bit < lax.axis_size("mp"):
@@ -1245,7 +1248,7 @@
             ((1, 1), F32),
         ],
         flops=unit,
-        limit=40 * MIB,
+        limit=28 * MIB,
     )
     shard_shape = (slots, 1, BLK, BLK)
     return (

time: 186 us -> 185 us (level)
  waiting for transfers between devices: 46.4 us -> 53.9 us
  Pallas kernels: 82.4 us -> 78.1 us
  starting transfers between devices: 32.3 us -> 30.3 us
    ppermute x32, waiting for transfers between devices: 46.4 us -> 53.9 us  [swap(): return lax.ppermute(value, axis, [(i, i ^ bit) for i in range(count)])]
    pallas_call x10, Pallas kernels: 82.4 us -> 78.1 us  [call(): pl.pallas_call(body, name=name, out_shape=results, in_specs=[pl.BlockSpec...]
    ppermute x32, starting transfers between devices: 32.3 us -> 30.3 us  [swap(): return lax.ppermute(value, axis, [(i, i ^ bit) for i in range(count)])]
  transfers between devices with their start and end apart: 32 -> 32, of which waited for: 14 -> 15; matrix products, arithmetic and copies ran while one was open for 9% -> 8% of each run, Pallas kernels for 32% -> 30%
where the time goes in v3:
time: 185 us
  Pallas kernels  78.1 us (42%)
  waiting for transfers between devices  53.9 us (29%)
  starting transfers between devices  30.3 us (16%)
  other arithmetic  14.1 us (8%)
  between operations  4.38 us (2%)
  local copies, waits for them, and re-layouts  3.98 us (2%)
    pallas_call x10, Pallas kernels, call(): pl.pallas_call(body, name=name, out_shape=results, in_specs=[pl.BlockSpec...  78.1 us
    ppermute x32, waiting for transfers between devices, swap(): return lax.ppermute(value, axis, [(i, i ^ bit) for i in range(count)])  53.9 us
    ppermute x32, starting transfers between devices, swap(): return lax.ppermute(value, axis, [(i, i ^ bit) for i in range(count)])  30.3 us
    convert_element_type x18, other arithmetic, plus(): return (left.astype(F32) + right.astype(F32)).astype(BF16)  12.2 us
  transfers between devices with their start and end apart: 32, of which 15 were waited for; matrix products, arithmetic and copies ran while one was open for 8% of the time, Pallas kernels for 30%

profile of v3, /device:TPU:0, one launch (start us, length us, event | category | flops | bytes accessed | tf_op | source)
XLA Modules:
  0.0 184.7 jit_solution(5821026850971440595)
XLA Ops:
  0.7 10.2 %attention_forward.1 = (bf16[512,1024]{1,0:T(8,128)(2,1)}, bf16[512,256]{1,0:T(8,128)(2,1)}, bf16[512,256]{1,0:T(8,128)(2,1)}, bf16[512,256]{1,0:T(8,128)(2,1)},...) custom-call(s32[2]{0:T(128)S(1)} %pad_add_fusion.3.refs_0_, ...), custom_call_target="tpu_custom_call" | custom-call | flops 5368709120 | tf_op jit(solution)/shard_map/attention_forward/pallas_call | solution.py:354
  13.9 2.9 %collective-permute-start.4 = (bf16[128,1024]{1,0:T(8,128)(2,1)S(1)}, bf16[128,1024]{1,0:T(8,128)(2,1)S(1)}, u32[]{:S(2)}, u32[]{:S(2)}) collective-permute-start(bf16[128,1024]{1,0:T(8,128)(2,1)S(1)} %add_convert_fusion.23), channel_id=1, source_target_pairs={{0,2},{1,3},{2,0},{3,1},{4,6},{5,7},{6,4},{7,5},{8,10},{9,11},{10,... | collective-permute-start | bytes 786440 | tf_op jit(solution)/shard_map/ppermute | solution.py:820
  18.6 5.2 %grad_of_act.1 = (bf16[512,1024]{1,0:T(8,128)(2,1)}, f32[512,1024]{1,0:T(8,128)}) custom-call(s32[2]{0:T(128)S(1)} %pad_add_fusion.3.refs_0_, s32[1,512]{1,0:T(1,128)} %bitcast.46, bf16[512,1024]{1,0:T(8,128)(2,1)} %refs_2_.4, bf16[1024,1024]{1,0:T(8,128)(2,1)} %refs_30_.1, bf16[128,1024]{1,0:T(8,128)(2,1)} %add_convert_fusion.22.refs_4_), custom_call_target="tpu_custom_call" | custom-call | flops 2147483648 | tf_op jit(solution)/shard_map/grad_of_act/pallas_call | solution.py:354
  25.5 6.3 %feed_forward_a.1 = (bf16[256,1024]{1,0:T(8,128)(2,1)S(1)}, bf16[256,1024]{1,0:T(8,128)(2,1)S(1)}, bf16[256,1024]{1,0:T(8,128)(2,1)S(1)}, bf16[128,1024]{1,0:T(8,128)(2,1)S(1)}, bf16[128,1024]{1,0:T(8,128)(2,1)S(1)}) custom-call(s32[2]{0:T(128)S(1)} %pad_add_fusion.3.refs_0_, s32[1,512]{1,0:T(1,128)S(1)} %bitcast.36, bf16[192,512]{1,0:T(8,128)(2,1)S(1)} %copy-done.31, ...), custom_call_target="tpu_custom_call" | custom-call | flops 4294967296 | tf_op jit(solution)/shard_map/feed_forward_a/pallas_call | solution.py:354
  37.1 6.3 %feed_forward_b.1 = (bf16[256,1024]{1,0:T(8,128)(2,1)S(1)}, bf16[256,1024]{1,0:T(8,128)(2,1)S(1)}, bf16[256,1024]{1,0:T(8,128)(2,1)S(1)}, bf16[128,1024]{1,0:T(8,128)(2,1)S(1)}, bf16[128,1024]{1,0:T(8,128)(2,1)S(1)}) custom-call(s32[2]{0:T(128)S(1)} %pad_add_fusion.3.refs_0_, s32[1,512]{1,0:T(1,128)S(1)} %bitcast.37, bf16[192,512]{1,0:T(8,128)(2,1)S(1)} %copy-done.31, ...), custom_call_target="tpu_custom_call" | custom-call | flops 4294967296 | tf_op jit(solution)/shard_map/feed_forward_b/pallas_call | solution.py:354
  46.5 7.2 %feed_weight_grads.1 = (bf16[80,128,128]{2,1,0:T(8,128)(2,1)}, bf16[32,128,128]{2,1,0:T(8,128)(2,1)S(1)}, bf16[32,128,128]{2,1,0:T(8,128)(2,1)S(1)}) custom-call(s32[2]{0:T(128)S(1)} %pad_add_fusion.3.refs_0_, s32[336]{0:T(512)S(1)} %pad_add_fusion.2.refs_1_, f32[4]{0:T(128)S(1)} %pad_maximum_fusion.refs_2_.refs_1_, bf16[256,1024]{1,0:T(8,128)(2,1)S(1)} %copy-done.38, ...), custom_call_target="tpu_custom_call" | custom-call | flops 4294967296 | tf_op jit(solution)/shard_map/feed_weight_grads/pallas_call | solution.py:354
  53.9 4.1 %collective-permute-done.13 = bf16[128,1024]{1,0:T(8,128)(2,1)S(1)} collective-permute-done((bf16[128,1024]{1,0:T(8,128)(2,1)S(1)}, bf16[128,1024]{1,0:T(8,128)(2,1)S(1)}, u32[]{:S(2)}, u32[]{:S(2)}) %collective-permute-start.13) | collective-permute-done | bytes 262176 | tf_op jit(solution)/shard_map/ppermute | solution.py:820
  60.6 20.1 %attention_backward.1 = (bf16[64,128,128]{2,1,0:T(8,128)(2,1)}, bf16[512,1024]{1,0:T(8,128)(2,1)}, bf16[512,1024]{1,0:T(8,128)(2,1)}, bf16[28,128,128]{2,1,0:T(8...) custom-call(s32[2]{0:T(128)S(1)} %pad_add_fusion.3.refs_0_, ...), custom_call_target="tpu_custom_call" | custom-call | flops 10737418240 | tf_op jit(solution)/shard_map/attention_backward/pallas_call | solution.py:354
  84.1 2.6 %add_convert_fusion.6 = (bf16[16,128,128]{2,1,0:T(8,128)(2,1)}, bf16[16,128,128]{2,1,0:T(8,128)(2,1)}) fusion(bf16[32,128,128]{2,1,0:T(8,128)(2,1)} %collective-permute-done.16, bf16[32,128,128]{2,1,0:T(8,128)(2,1)S(1)} %get-tuple-element.121), kind=kLoop, calls=%fused_computation.6 | loop fusion | flops 2097152 | bytes 3145728 | tf_op jit(solution)/shard_map/convert_element_type | solution.py:824
  91.2 6.1 %collective-permute-done.19 = bf16[16,128,128]{2,1,0:T(8,128)(2,1)} collective-permute-done((bf16[16,128,128]{2,1,0:T(8,128)(2,1)}, bf16[16,128,128]{2,1,0:T(8,128)(2,1)}, u32[]{:S(2)}, u32[]{:S(2)}) %collective-permute-start.19) | collective-permute-done | bytes 524320 | tf_op jit(solution)/shard_map/ppermute | solution.py:820
  99.4 5.0 %collective-permute-done.18 = bf16[28,128,128]{2,1,0:T(8,128)(2,1)} collective-permute-done((bf16[28,128,128]{2,1,0:T(8,128)(2,1)}, bf16[28,128,128]{2,1,0:T(8,128)(2,1)}, u32[]{:S(2)}, u32[]{:S(2)}) %collective-permute-start.18) | collective-permute-done | bytes 917536 | tf_op jit(solution)/shard_map/ppermute | solution.py:820
  111.9 2.7 %collective-permute-start.26 = (bf16[8,128,128]{2,1,0:T(8,128)(2,1)S(1)}, bf16[8,128,128]{2,1,0:T(8,128)(2,1)S(1)}, u32[]{:S(2)}, u32[]{:S(2)}) collective-permute-start(bf16[8,128,128]{2,1,0:T(8,128)(2,1)S(1)} %get-tuple-element.193), channel_id=1, source_target_pairs={{0,16},{4,20},{8,24},{12,28},{16,0},{20,4},{24,8},{28,12},{1,17},{... | collective-permute-start | bytes 786440 | tf_op jit(solution)/shard_map/ppermute | solution.py:820
  114.6 3.8 %collective-permute-done.21 = bf16[20,128,128]{2,1,0:T(8,128)(2,1)S(1)} collective-permute-done((bf16[20,128,128]{2,1,0:T(8,128)(2,1)}, bf16[20,128,128]{2,1,0:T(8,128)(2,1)S(1)}, u32[]{:S(2)}, u32[]{:S(2)}) %collective-permute-start.21) | collective-permute-done | bytes 655392 | tf_op jit(solution)/shard_map/ppermute | solution.py:820
  120.2 5.0 %collective-permute-done.20 = bf16[14,128,128]{2,1,0:T(8,128)(2,1)S(1)} collective-permute-done((bf16[14,128,128]{2,1,0:T(8,128)(2,1)S(1)}, bf16[14,128,128]{2,1,0:T(8,128)(2,1)S(1)}, u32[]{:S(2)}, u32[]{:S(2)}) %collective-permute-start.20) | collective-permute-done | bytes 458784 | tf_op jit(solution)/shard_map/ppermute | solution.py:820
  125.7 9.3 %collective-permute-done.24 = bf16[10,128,128]{2,1,0:T(8,128)(2,1)S(1)} collective-permute-done((bf16[10,128,128]{2,1,0:T(8,128)(2,1)S(1)}, bf16[10,128,128]{2,1,0:T(8,128)(2,1)S(1)}, u32[]{:S(2)}, u32[]{:S(2)}) %collective-permute-start.24) | collective-permute-done | bytes 327712 | tf_op jit(solution)/shard_map/ppermute | solution.py:820
  138.2 2.5 %collective-permute-start.28 = (bf16[5,128,128]{2,1,0:T(8,128)(2,1)S(1)}, bf16[5,128,128]{2,1,0:T(8,128)(2,1)S(1)}, u32[]{:S(2)}, u32[]{:S(2)}) collective-permute-start(bf16[5,128,128]{2,1,0:T(8,128)(2,1)S(1)} %get-tuple-element.199), channel_id=1, source_target_pairs={{0,16},{4,20},{8,24},{12,28},{16,0},{20,4},{24,8},{28,12},{1,17},{... | collective-permute-start | bytes 491528 | tf_op jit(solution)/shard_map/ppermute | solution.py:820
  140.9 7.3 %layer_outputs.1 = (f32[512,1024]{1,0:T(8,128)}, f32[512,1024]{1,0:T(8,128)}, f32[8,1024]{1,0:T(8,128)S(1)}) custom-call(s32[2]{0:T(128)S(1)} %pad_add_fusion.3.refs_0_, f32[4]{0:T(128)S(1)} %copy-done.18, s32[1,512]{1,0:T(1,128)S(1)} %bitcast.38, bf16[192,512]{1,0:T(8,128)(2,1)S(1)} %copy-done.32, bf16[512,1024]{1,0:T(8,128)(2,1)S(1)} %copy-done.20, ...), custom_call_target="tpu_custom_call" | custom-call | flops 2147483648 | tf_op jit(solution)/shard_map/layer_outputs/pallas_call | solution.py:354
  148.2 6.1 %collective-permute-done.28.refs_7_ = bf16[5,128,128]{2,1,0:T(8,128)(2,1)S(1)} collective-permute-done((bf16[5,128,128]{2,1,0:T(8,128)(2,1)S(1)}, bf16[5,128,128]{2,1,0:T(8,128)(2,1)S(1)}, u32[]{:S(2)}, u32[]{:S(2)}) %collective-permute-start.28) | collective-permute-done | bytes 163872 | tf_op jit(solution)/shard_map/ppermute | solution.py:820
  154.3 4.2 %collect.1 = (f32[24,128,128]{2,1,0:T(8,128)S(1)}, f32[8,128]{1,0:T(8,128)S(1)}) custom-call(s32[2]{0:T(128)S(1)} %pad_add_fusion.3.refs_0_, s32[192]{0:T(256)S(1)} %compare_select_fusion.1.refs_1_, bf16[8,128,128]{2,1,0:T(8,128)(2,1)S(1)} %get-tuple-element.192.refs_2_, bf16[8,128,128]{2,1,0:T(8,128)(2,1)S(1)} %collective-permute-done.26.refs_3_, ...), custom_call_target="tpu_custom_call" | custom-call | flops 1073741824 | tf_op jit(solution)/shard_map/collect/pallas_call | solution.py:354
  161.0 2.3 %collective-permute-done.31 = f32[8,128]{1,0:T(8,128)S(1)} collective-permute-done((f32[8,128]{1,0:T(8,128)S(1)}, f32[8,128]{1,0:T(8,128)S(1)}, u32[]{:S(2)}, u32[]{:S(2)}) %collective-permute-start.31) | collective-permute-done | bytes 4128 | tf_op jit(solution)/shard_map/ppermute | solution.py:820
  164.6 2.7 %collective-permute-done.32 = f32[8,1024]{1,0:T(8,128)S(1)} collective-permute-done((f32[8,1024]{1,0:T(8,128)S(1)}, f32[8,1024]{1,0:T(8,128)S(1)}, u32[]{:S(2)}, u32[]{:S(2)}) %collective-permute-start.32) | collective-permute-done | bytes 32800 | tf_op jit(solution)/shard_map/ppermute | solution.py:820
  167.5 3.9 %collective-permute-done.33 = f32[8,1024]{1,0:T(8,128)S(1)} collective-permute-done((f32[8,1024]{1,0:T(8,128)S(1)}, f32[8,1024]{1,0:T(8,128)S(1)}, u32[]{:S(2)}, u32[]{:S(2)}) %collective-permute-start.33) | collective-permute-done | bytes 32800 | tf_op jit(solution)/shard_map/ppermute | solution.py:820
  171.4 3.1 %rotate.1.refs_9_ = f32[24,128,128]{2,1,0:T(8,128)S(1)} custom-call(s32[2]{0:T(128)S(1)} %pad_add_fusion.3.refs_0_, f32[24,128]{1,0:T(8,128)S(1)} %bitcast.30, f32[24,128]{1,0:T(8,128)S(1)} %bitcast.32, f32[24,128,128]{2,1,0:T(8,128)S(1)} %get-tuple-element.148.refs_3_.refs_8_), custom_call_target="tpu_custom_call" | custom-call | flops 1073741824 | tf_op jit(solution)/shard_map/rotate/pallas_call | solution.py:354
  176.3 8.2 %update.1 = (f32[24,128,128]{2,1,0:T(8,128)}, f32[24,128,128]{2,1,0:T(8,128)}, f32[24,128,128]{2,1,0:T(8,128)}, f32[24,128,128]{2,1,0:T(8,128)}, bf16[24,128,128...) custom-call(s32[2]{0:T(128)S(1)} %pad_add_fusion.3.refs_0_, ...), custom_call_target="tpu_custom_call" | custom-call | flops 1073741824 | tf_op jit(solution)/shard_map/update/pallas_call | solution.py:354
  (205 shorter events, 44.0 us)
Async XLA Ops:
  11.5 5.3 %collective-permute-start.5 = (bf16[128,1024]{1,0:T(8,128)(2,1)}, bf16[128,1024]{1,0:T(8,128)(2,1)S(1)}, u32[]{:S(2)}, u32[]{:S(2)}) collective-permute-start(bf16[128,1024]{1,0:T(8,128)(2,1)} %get-tuple-element.93), channel_id=1, source_target_pairs={{0,1},{1,0},{2,3},{3,2},{4,5},{5,4},{6,7},{7,6},{8,9},{9,8},{10,11... | collective-permute-start | bytes 786440 | tf_op jit(solution)/shard_map/ppermute | solution.py:820
  13.9 9.9 %collective-permute-start.4 = (bf16[128,1024]{1,0:T(8,128)(2,1)S(1)}, bf16[128,1024]{1,0:T(8,128)(2,1)S(1)}, u32[]{:S(2)}, u32[]{:S(2)}) collective-permute-start(bf16[128,1024]{1,0:T(8,128)(2,1)S(1)} %add_convert_fusion.23), channel_id=1, source_target_pairs={{0,2},{1,3},{2,0},{3,1},{4,6},{5,7},{6,4},{7,5},{8,10},{9,11},{10,... | collective-permute-start | bytes 786440 | tf_op jit(solution)/shard_map/ppermute | solution.py:820
  24.1 9.4 %collective-permute-start.7 = (bf16[128,1024]{1,0:T(8,128)(2,1)S(1)}, bf16[128,1024]{1,0:T(8,128)(2,1)S(1)}, u32[]{:S(2)}, u32[]{:S(2)}) collective-permute-start(bf16[128,1024]{1,0:T(8,128)(2,1)S(1)} %copy-done.44), channel_id=1, source_target_pairs={{0,2},{1,3},{2,0},{3,1},{4,6},{5,7},{6,4},{7,5},{8,10},{9,11},{10,... | collective-permute-start | bytes 786440 | tf_op jit(solution)/shard_map/ppermute | solution.py:820
  36.7 7.0 %collective-permute-start.9 = (bf16[128,1024]{1,0:T(8,128)(2,1)S(1)}, bf16[128,1024]{1,0:T(8,128)(2,1)S(1)}, u32[]{:S(2)}, u32[]{:S(2)}) collective-permute-start(bf16[128,1024]{1,0:T(8,128)(2,1)S(1)} %get-tuple-element.98), channel_id=1, source_target_pairs={{0,1},{1,0},{2,3},{3,2},{4,5},{5,4},{6,7},{7,6},{8,9},{9,8},{10,11... | collective-permute-start | bytes 786440 | tf_op jit(solution)/shard_map/ppermute | solution.py:820
  43.9 9.9 %collective-permute-start.10 = (bf16[128,1024]{1,0:T(8,128)(2,1)S(1)}, bf16[128,1024]{1,0:T(8,128)(2,1)S(1)}, u32[]{:S(2)}, u32[]{:S(2)}) collective-permute-start(bf16[128,1024]{1,0:T(8,128)(2,1)S(1)} %add_convert_fusion.19), channel_id=1, source_target_pairs={{0,2},{1,3},{2,0},{3,1},{4,6},{5,7},{6,4},{7,5},{8,10},{9,11},{10,... | collective-permute-start | bytes 786440 | tf_op jit(solution)/shard_map/ppermute | solution.py:820
  45.3 12.8 %collective-permute-start.13 = (bf16[128,1024]{1,0:T(8,128)(2,1)S(1)}, bf16[128,1024]{1,0:T(8,128)(2,1)S(1)}, u32[]{:S(2)}, u32[]{:S(2)}) collective-permute-start(bf16[128,1024]{1,0:T(8,128)(2,1)S(1)} %add_convert_fusion.18.refs_10_), channel_id=1, source_target_pairs={{0,2},{1,3},{2,0},{3,1},{4,6},{5,7},{6,4},{7,5},{8,10},{9,11},{10,... | collective-permute-start | bytes 786440 | tf_op jit(solution)/shard_map/ppermute | solution.py:820
  53.9 5.9 %collective-permute-start.12 = (bf16[128,1024]{1,0:T(8,128)(2,1)S(1)}, bf16[128,1024]{1,0:T(8,128)(2,1)S(1)}, u32[]{:S(2)}, u32[]{:S(2)}) collective-permute-start(bf16[128,1024]{1,0:T(8,128)(2,1)S(1)} %add_convert_fusion.17.refs_11_.refs_12_), channel_id=1, source_target_pairs={{0,1},{1,0},{2,3},{3,2},{4,5},{5,4},{6,7},{7,6},{8,9},{9,8},{10,11... | collective-permute-start | bytes 786440 | tf_op jit(solution)/shard_map/ppermute | solution.py:820
  58.2 25.9 %collective-permute-start.16 = (bf16[32,128,128]{2,1,0:T(8,128)(2,1)S(1)}, bf16[32,128,128]{2,1,0:T(8,128)(2,1)}, u32[]{:S(2)}, u32[]{:S(2)}) collective-permute-start(bf16[32,128,128]{2,1,0:T(8,128)(2,1)S(1)} %get-tuple-element.119), channel_id=1, source_target_pairs={{0,4},{4,0},{8,12},{12,8},{16,20},{20,16},{24,28},{28,24},{1,5},{5... | collective-permute-start | bytes 3145736 | tf_op jit(solution)/shard_map/ppermute | solution.py:820
  80.7 10.5 %collective-permute-start.15 = (bf16[512,1024]{1,0:T(8,128)(2,1)}, bf16[512,1024]{1,0:T(8,128)(2,1)}, u32[]{:S(2)}, u32[]{:S(2)}) collective-permute-start(bf16[512,1024]{1,0:T(8,128)(2,1)} %get-tuple-element.118), channel_id=1, source_target_pairs={{0,1},{1,0},{2,3},{3,2},{4,5},{5,4},{6,7},{7,6},{8,9},{9,8},{10,11... | collective-permute-start | bytes 3145736 | tf_op jit(solution)/shard_map/ppermute | solution.py:820
  80.9 23.5 %collective-permute-start.18 = (bf16[28,128,128]{2,1,0:T(8,128)(2,1)}, bf16[28,128,128]{2,1,0:T(8,128)(2,1)}, u32[]{:S(2)}, u32[]{:S(2)}) collective-permute-start(bf16[28,128,128]{2,1,0:T(8,128)(2,1)} %get-tuple-element.124), channel_id=1, source_target_pairs={{0,4},{4,0},{8,12},{12,8},{16,20},{20,16},{24,28},{28,24},{1,5},{5... | collective-permute-start | bytes 2752520 | tf_op jit(solution)/shard_map/ppermute | solution.py:820
  82.2 15.1 %collective-permute-start.19 = (bf16[16,128,128]{2,1,0:T(8,128)(2,1)}, bf16[16,128,128]{2,1,0:T(8,128)(2,1)}, u32[]{:S(2)}, u32[]{:S(2)}) collective-permute-start(bf16[16,128,128]{2,1,0:T(8,128)(2,1)} %get-tuple-element.125), channel_id=1, source_target_pairs={{0,8},{4,12},{8,0},{12,4},{16,24},{20,28},{24,16},{28,20},{1,9},{5... | collective-permute-start | bytes 1572872 | tf_op jit(solution)/shard_map/ppermute | solution.py:820
  86.7 21.0 %collective-permute-start.22 = (bf16[16,128,128]{2,1,0:T(8,128)(2,1)}, bf16[16,128,128]{2,1,0:T(8,128)(2,1)}, u32[]{:S(2)}, u32[]{:S(2)}) collective-permute-start(bf16[16,128,128]{2,1,0:T(8,128)(2,1)} %get-tuple-element.187), channel_id=1, source_target_pairs={{0,8},{4,12},{8,0},{12,4},{16,24},{20,28},{24,16},{28,20},{1,9},{5... | collective-permute-start | bytes 1572872 | tf_op jit(solution)/shard_map/ppermute | solution.py:820
  89.6 28.7 %collective-permute-start.21 = (bf16[20,128,128]{2,1,0:T(8,128)(2,1)}, bf16[20,128,128]{2,1,0:T(8,128)(2,1)S(1)}, u32[]{:S(2)}, u32[]{:S(2)}) collective-permute-start(bf16[20,128,128]{2,1,0:T(8,128)(2,1)} %get-tuple-element.131), channel_id=1, source_target_pairs={{0,4},{4,0},{8,12},{12,8},{16,20},{20,16},{24,28},{28,24},{1,5},{5... | collective-permute-start | bytes 1966088 | tf_op jit(solution)/shard_map/ppermute | solution.py:820
  98.6 26.8 %collective-permute-start.25 = (bf16[8,128,128]{2,1,0:T(8,128)(2,1)S(1)}, bf16[8,128,128]{2,1,0:T(8,128)(2,1)S(1)}, u32[]{:S(2)}, u32[]{:S(2)}) collective-permute-start(bf16[8,128,128]{2,1,0:T(8,128)(2,1)S(1)} %get-tuple-element.195), channel_id=1, source_target_pairs={{0,4},{4,0},{8,12},{12,8},{16,20},{20,16},{24,28},{28,24},{1,5},{5... | collective-permute-start | bytes 786440 | tf_op jit(solution)/shard_map/ppermute | solution.py:820
  105.8 19.3 %collective-permute-start.20 = (bf16[14,128,128]{2,1,0:T(8,128)(2,1)S(1)}, bf16[14,128,128]{2,1,0:T(8,128)(2,1)S(1)}, u32[]{:S(2)}, u32[]{:S(2)}) collective-permute-start(bf16[14,128,128]{2,1,0:T(8,128)(2,1)S(1)} %get-tuple-element.188), channel_id=1, source_target_pairs={{0,8},{4,12},{8,0},{12,4},{16,24},{20,28},{24,16},{28,20},{1,9},{5... | collective-permute-start | bytes 1376264 | tf_op jit(solution)/shard_map/ppermute | solution.py:820
  109.3 27.9 %collective-permute-start.17 = (bf16[512,1024]{1,0:T(8,128)(2,1)S(1)}, bf16[512,1024]{1,0:T(8,128)(2,1)S(1)}, u32[]{:S(2)}, u32[]{:S(2)}) collective-permute-start(bf16[512,1024]{1,0:T(8,128)(2,1)S(1)} %add_convert_fusion.5), channel_id=1, source_target_pairs={{0,2},{1,3},{2,0},{3,1},{4,6},{5,7},{6,4},{7,5},{8,10},{9,11},{10,... | collective-permute-start | bytes 3145736 | tf_op jit(solution)/shard_map/ppermute | solution.py:820
  111.9 13.5 %collective-permute-start.26 = (bf16[8,128,128]{2,1,0:T(8,128)(2,1)S(1)}, bf16[8,128,128]{2,1,0:T(8,128)(2,1)S(1)}, u32[]{:S(2)}, u32[]{:S(2)}) collective-permute-start(bf16[8,128,128]{2,1,0:T(8,128)(2,1)S(1)} %get-tuple-element.193), channel_id=1, source_target_pairs={{0,16},{4,20},{8,24},{12,28},{16,0},{20,4},{24,8},{28,12},{1,17},{... | collective-permute-start | bytes 786440 | tf_op jit(solution)/shard_map/ppermute | solution.py:820
  118.5 16.4 %collective-permute-start.24 = (bf16[10,128,128]{2,1,0:T(8,128)(2,1)S(1)}, bf16[10,128,128]{2,1,0:T(8,128)(2,1)S(1)}, u32[]{:S(2)}, u32[]{:S(2)}) collective-permute-start(bf16[10,128,128]{2,1,0:T(8,128)(2,1)S(1)} %get-tuple-element.191), channel_id=1, source_target_pairs={{0,8},{4,12},{8,0},{12,4},{16,24},{20,28},{24,16},{28,20},{1,9},{5... | collective-permute-start | bytes 983048 | tf_op jit(solution)/shard_map/ppermute | solution.py:820
  125.3 11.9 %collective-permute-start.23 = (bf16[7,128,128]{2,1,0:T(8,128)(2,1)S(1)}, bf16[7,128,128]{2,1,0:T(8,128)(2,1)S(1)}, u32[]{:S(2)}, u32[]{:S(2)}) collective-permute-start(bf16[7,128,128]{2,1,0:T(8,128)(2,1)S(1)} %get-tuple-element.197), channel_id=1, source_target_pairs={{0,16},{4,20},{8,24},{12,28},{16,0},{20,4},{24,8},{28,12},{1,17},{... | collective-permute-start | bytes 688136 | tf_op jit(solution)/shard_map/ppermute | solution.py:820
  137.7 16.6 %collective-permute-start.29 = (bf16[4,128,128]{2,1,0:T(8,128)(2,1)S(1)}, bf16[4,128,128]{2,1,0:T(8,128)(2,1)S(1)}, u32[]{:S(2)}, u32[]{:S(2)}) collective-permute-start(bf16[4,128,128]{2,1,0:T(8,128)(2,1)S(1)} %get-tuple-element.201), channel_id=1, source_target_pairs={{0,16},{4,20},{8,24},{12,28},{16,0},{20,4},{24,8},{28,12},{1,17},{... | collective-permute-start | bytes 393224 | tf_op jit(solution)/shard_map/ppermute | solution.py:820
  138.2 16.1 %collective-permute-start.28 = (bf16[5,128,128]{2,1,0:T(8,128)(2,1)S(1)}, bf16[5,128,128]{2,1,0:T(8,128)(2,1)S(1)}, u32[]{:S(2)}, u32[]{:S(2)}) collective-permute-start(bf16[5,128,128]{2,1,0:T(8,128)(2,1)S(1)} %get-tuple-element.199), channel_id=1, source_target_pairs={{0,16},{4,20},{8,24},{12,28},{16,0},{20,4},{24,8},{28,12},{1,17},{... | collective-permute-start | bytes 491528 | tf_op jit(solution)/shard_map/ppermute | solution.py:820
  163.4 4.0 %collective-permute-start.32 = (f32[8,1024]{1,0:T(8,128)S(1)}, f32[8,1024]{1,0:T(8,128)S(1)}, u32[]{:S(2)}, u32[]{:S(2)}) collective-permute-start(f32[8,1024]{1,0:T(8,128)S(1)} %pad_add_fusion), channel_id=1, source_target_pairs={{0,4},{4,0},{8,12},{12,8},{16,20},{20,16},{24,28},{28,24},{1,5},{5... | collective-permute-start | bytes 98312 | tf_op jit(solution)/shard_map/ppermute | solution.py:820
  167.4 4.0 %collective-permute-start.33 = (f32[8,1024]{1,0:T(8,128)S(1)}, f32[8,1024]{1,0:T(8,128)S(1)}, u32[]{:S(2)}, u32[]{:S(2)}) collective-permute-start(f32[8,1024]{1,0:T(8,128)S(1)} %fusion.4), channel_id=1, source_target_pairs={{0,8},{4,12},{8,0},{12,4},{16,24},{20,28},{24,16},{28,20},{1,9},{5... | collective-permute-start | bytes 98312 | tf_op jit(solution)/shard_map/ppermute | solution.py:820
  171.4 4.9 %collective-permute-start.34 = (f32[8,1024]{1,0:T(8,128)S(1)}, f32[8,1024]{1,0:T(8,128)S(1)}, u32[]{:S(2)}, u32[]{:S(2)}) collective-permute-start(f32[8,1024]{1,0:T(8,128)S(1)} %add.162), channel_id=1, source_target_pairs={{0,16},{4,20},{8,24},{12,28},{16,0},{20,4},{24,8},{28,12},{1,17},{... | collective-permute-start | bytes 98312 | tf_op jit(solution)/shard_map/ppermute | solution.py:820
  (59 other events, 540.1 us)
